TPU v7x, 256 devices: a whole 4x4x8 slice. The times are simulated.
256 devices in a mesh: seq: 64 (over y, x_lo, z), filt: 4 (over x_hi, core).
Axes of the slice: x: 4 (x_hi: 2, x_lo: 2; x = x_hi * 2 + x_lo), y: 4, z: 8, core: 2. Of those that a mesh axis runs over, the one named last changes fastest.
Arguments:
- inputs: bfloat16 [8192, 1024], P('seq'), may hold values from -16 to 16
- cotangent: bfloat16 [8192, 1024], P('seq'), may hold values from -6 to 6
- filters: bfloat16 [12, 8192], replicated, may hold values from -0.0625 to 0.0625
- projections: bfloat16 [12, 1024, 1024], P('filt'), may hold values from -0.1875 to 0.1875
Outputs:
- input_grad: bfloat16 [8192, 1024], P('seq', 'filt')
- projection_grad: bfloat16 [12, 1024, 1024], P('filt', 'seq')
All inputs are finite; a program needn't handle non-finite values.
Results may differ from a plain program's by a relative error of at most 0.015.
Values may be sent and summed in bfloat16 or wider, within the bound.
A program may use at most 192 MiB of HBM per device.

v0:
```python
import jax
import jax.numpy as jnp
from jax import lax
from jax.sharding import PartitionSpec as P


def lag_block(padded, first, start, count, rows, length):
    offset = start - first - rows + 1 + length
    window = lax.dynamic_slice_in_dim(padded, offset, count + rows - 1, 1)
    window = jnp.concatenate([window, jnp.zeros((window.shape[0], 1), window.dtype)], axis=1)
    period = count + rows
    tiled = jnp.tile(window, (1, rows + 1))[:, : rows * (period + 1)]
    hankel = tiled.reshape(window.shape[0], rows, period + 1)[:, :, :count]
    return hankel[:, ::-1, :]


def per_device(inputs, cotangent, filters, projections):
    rows = inputs.shape[0]
    width = inputs.shape[1]
    owned = projections.shape[0]
    length = filters.shape[1]
    first = lax.axis_index("seq") * rows
    filt_pos = lax.axis_index("filt")
    own_taps = lax.dynamic_slice_in_dim(filters, filt_pos * owned, owned, 0)
    empty = jnp.zeros((owned, rows, width), jnp.float32)
    piece = lax.all_gather(cotangent, "seq", axis=0, tiled=True)
    start = jnp.int32(0)
    padded = jnp.concatenate(
        [jnp.zeros((own_taps.shape[0], length), own_taps.dtype), own_taps], axis=1
    )
    count = piece.shape[0]

    def compute(running):
        block = lag_block(padded, first, start, count, rows, length)
        return jnp.einsum("kac,cd->kad", block, piece, preferred_element_type=jnp.float32)

    whole = lax.cond(start + count > first, compute, lambda running: running, empty)
    corr = whole.astype(jnp.bfloat16)
    partial_grad = jnp.einsum("kac,kec->ae", corr, projections, preferred_element_type=jnp.float32)
    input_grad = lax.psum_scatter(
        partial_grad.astype(jnp.bfloat16), "filt", scatter_dimension=1, tiled=True
    )
    scale = float(length) ** (-0.5)
    summed = lax.psum_scatter(
        jnp.einsum("ad,kae->dke", inputs, corr, preferred_element_type=jnp.float32) * scale,
        "seq",
        scatter_dimension=0,
        tiled=True,
    )
    projection_grad = jnp.transpose(summed, (1, 0, 2)).astype(jnp.bfloat16)
    return (input_grad, projection_grad)


def solution(mesh):
    placed = (P("seq", None), P("seq", None), P(), P("filt", None, None))
    return jax.shard_map(
        per_device,
        mesh=mesh,
        in_specs=placed,
        out_specs=(P("seq", "filt"), P("filt", "seq", None)),
        check_vma=False,
    )
```

profile of v0, /device:TPU:4, one launch (start us, length us, event | category | flops | bytes accessed | tf_op | source)
XLA Modules:
  0.0 926.9 jit_solution(7245532473312365448)
XLA Ops:
  7.2 0.0 copy-start
  7.2 0.0 all-gather.2.cloned.1.call-start
  7.2 0.7 all-gather.2.cloned.1.call-update
  7.9 0.0 reduce-scatter.2.cloned.1.call-start
  8.0 1.3 dynamic-slice
  9.9 335.4 %all-gather.2.cloned.1.call-done = bf16[8192,1024]{1,0:T(8,128)(2,1)} async-done(((bf16[128,1024]{1,0:T(8,128)(2,1)}), bf16[8192,1024]{1,0:T(8,128)(2,1)}) %all-gather.2.cloned.1.call-update) | async-done | bytes 16777232 | tf_op jit(solution)/shard_map/all_gather | solution.py:26
  345.3 152.3 %conditional.1 = (bf16[3,128,1024]{2,1,0:T(8,128)(2,1)S(1)}) conditional(s32[]{:T(128)} %convert_element_type.20, () %tuple.30, (s32[]{:T(128)}, bf16[12,8192]{1,0:T(8,128)(2,1)}, s32[]{:T(128)}, bf16[8192,1024]{1,0:T(8,128)(2,1)}) %tuple.31), branch_computations={%region_0.0_spmd, %region_1.0_spmd} | conditional | flops 6442844160 | bytes 107030368 | solution.py:37
  345.3 1.0 constant_dynamic-slice_fusion
  346.3 0.3 pad_dynamic-slice_fusion
  346.7 0.4 broadcast_bitcast_fusion
  347.1 3.3 copy.15
  350.4 4.7 slice.10
  355.1 18.4 %reshape.17 = bf16[3195264]{0:T(1024)(128)(2,1)} reshape(bf16[3,1065088]{1,0:T(4,128)(2,1)} %slice.10) | data formatting | bytes 12781056 | tf_op jit(solution)/shard_map/cond
  373.5 16.0 %reshape.12 = bf16[3,128,8321]{2,1,0:T(8,128)(2,1)} reshape(bf16[3195264]{0:T(1024)(128)(2,1)} %reshape.17) | data formatting | bytes 12781056 | tf_op jit(solution)/shard_map/cond/branch_1_fun/reshape | solution.py:13
  389.5 6.1 slice.11
  395.6 89.7 %rev.4 = bf16[3,128,8192]{2,1,0:T(8,128)(2,1)} reverse(bf16[3,128,8192]{2,1,0:T(8,128)(2,1)} %slice.11), dimensions={1} | reverse | bytes 12582912 | tf_op jit(solution)/shard_map/cond/branch_1_fun/rev | solution.py:14
  485.4 12.3 %fusion.2 = bf16[3,128,1024]{2,1,0:T(8,128)(2,1)S(1)} fusion(bf16[3,128,8192]{2,1,0:T(8,128)(2,1)} %rev.4, bf16[8192,1024]{1,0:T(8,128)(2,1)} %get-tuple-element.51), kind=kOutput, calls=%fused_computation.3 | convolution fusion | flops 6442844160 | bytes 23855104 | tf_op jit(solution)/shard_map/cond/branch_1_fun/kac,cd->kad/dot_general | solution.py:35
  497.6 5.7 fusion.5
  503.3 0.0 reduce-scatter.2.cloned.1.call-update
  503.3 6.4 multiply_bitcast_fusion
  509.7 18.4 %copy.12 = f32[1024,3,1024]{2,1,0:T(4,128)} copy(f32[1024,3,1024]{0,2,1:T(8,128)} %multiply_bitcast_fusion) | data formatting | bytes 25165824 | tf_op jit(solution)/shard_map/mul | solution.py:45
  528.2 390.3 %all-reduce.4 = bf16[1024,3,1024]{2,1,0:T(4,128)(2,1)} all-reduce(f32[1024,3,1024]{2,1,0:T(4,128)} %copy.12), channel_id=3, replica_groups=mesh['seq'=64,'filt'=4] {'seq'}, use_global_device_ids=true, to_apply=%region_3.0.clone | all-reduce | flops 3145728 | bytes 18874368
  918.5 0.9 fusion.7
  919.4 0.7 copy.13
  (3 shorter events, 0.0 us)
Async XLA Ops:
  7.2 496.2 %copy-start = (bf16[128,1024]{1,0:T(8,128)(2,1)S(1)}, bf16[128,1024]{1,0:T(8,128)(2,1)}, u32[]{:S(2)}) copy-start(bf16[128,1024]{1,0:T(8,128)(2,1)} %param.6) | copy-start | bytes 786436
  7.2 338.1 %all-gather.2.cloned.1.call-start = ((), (), s32[]{:S(2)}) async-start(), calls=%async_computation.1 | async-start | bytes 17039360 | tf_op jit(solution)/shard_map/all_gather | solution.py:26
  7.9 912.2 %reduce-scatter.2.cloned.1.call-start = ((), (), s32[]{:S(2)}) async-start(), calls=%async_computation.2 | async-start | bytes 327680 | tf_op jit(solution)/shard_map/reduce_scatter | solution.py:40
Sparse Core Ops, SparseCore 0:
  9.8 335.4 all-gather.1
  503.5 144.3 reduce-scatter.1
where the time goes:
time: 938 us; the launch traced here: 927 us
  blocking collectives  390 us (42%)
  waiting for transfers between devices  336 us (36%)
  local copies, waits for them, and re-layouts  161 us (17%)
  matrix products  24.3 us (3%)
  between operations  14.7 us (2%)
    unnamed x1, blocking collectives  390 us
    all_gather x1, waiting for transfers between devices, per_device(): piece = lax.all_gather(cotangent, 'seq', axis=0, tiled=True)  335 us
    rev x1, local copies, waits for them, and re-layouts, lag_block(): return hankel[:, ::-1, :]  89.7 us
    cond x3, local copies, waits for them, and re-layouts  22.1 us
  transfers between devices with their start and end apart: 2, of which 1 were waited for; matrix products, arithmetic and copies ran while one was open for 3% of the time, Pallas kernels for 0%

commit v1 on v0

v1 whole, which is shorter than its diff:
```python
import functools

import jax
import jax.numpy as jnp
from jax import lax
from jax.experimental import pallas as pl
from jax.experimental.pallas import tpu as pltpu
from jax.sharding import PartitionSpec as P

MESH = pl.DeviceIdType.MESH
F32 = jnp.float32
BF16 = jnp.bfloat16
B = 128
ORDER = (0, 1, -1, 2, -2, 3, -3, 4)


def kernel(
    x_ref, g_ref, f_ref, p_ref, ig_ref, pg_ref,
    taps, hank, gl, g2, acc, corr, xs, xt, pn, pgb, pgr, pgs, pga, pgo,
    igs, igr, igo, igc, igd,
    ga_s, ga_r, gr_s, gr_r, gs_s, gs_r, xa_s, xa_r, xs_s, xs_r, loc,
    pr_s, pr_r, pa_s, pa_r, is_s, is_r, id_s, id_r,
):
    seq = lax.axis_index("seq")
    filt = lax.axis_index("filt")
    q, z = lax.div(seq, 8), lax.rem(seq, 8)
    xh, core = lax.div(filt, 2), lax.rem(filt, 2)
    sib = (seq, xh * 2 + 1 - core)
    up = (q * 8 + lax.rem(z + 1, 8), filt)
    down = (q * 8 + lax.rem(z + 7, 8), filt)

    def plane(dx, dq):
        return (lax.rem(q + dq, 8) * 8 + z, lax.rem(xh + dx, 2) * 2 + core)

    def remote(src, dst, send, recv, to):
        return pltpu.make_async_remote_copy(
            src_ref=src, dst_ref=dst, send_sem=send, recv_sem=recv,
            device_id=to, device_id_type=MESH,
        )

    sent = []

    def go(copy):
        copy.start()
        sent.append(copy)

    barrier = pltpu.get_barrier_semaphore()
    partners = [sib, up, down] + [plane(r // 8, r % 8) for r in range(1, 16)]
    for to in partners:
        pl.semaphore_signal(barrier, inc=1, device_id=to, device_id_type=MESH)

    p_copies = [
        pltpu.make_async_copy(
            p_ref.at[k, :, pl.ds(pl.multiple_of(q * B, B), B)],
            pn.at[:, pl.ds(k * B, B)],
            loc.at[k],
        )
        for k in range(3)
    ]
    for c in p_copies:
        c.start()
    pick = jnp.where(
        lax.broadcasted_iota(jnp.int32, (8, 12), 1)
        == lax.broadcasted_iota(jnp.int32, (8, 12), 0) + 3 * filt,
        1.0, 0.0,
    ).astype(BF16)
    taps[...] = jnp.dot(pick, f_ref[...], preferred_element_type=F32)
    g2[...] = jnp.zeros_like(g2)
    rows = pl.ds(pl.multiple_of(core * 64, 64), 64)
    gl[0, core, q] = g_ref[rows, pl.ds(pl.multiple_of(q * B, B), B)]

    pl.semaphore_wait(barrier, len(partners))

    a2a = []
    for r in range(1, 8):
        col = pl.ds(pl.multiple_of(lax.rem(q + r, 8) * B, B), B)
        a2a.append(
            remote(g_ref.at[rows, col], gl.at[0, core, q], ga_s.at[r], ga_r.at[r], plane(0, r))
        )
        go(a2a[-1])

    for t in range(8):
        flip = x_ref[:, t * B:(t + 1) * B].T
        for zz in range(8):
            xs[zz, t * 16:(t + 1) * 16, :] = flip[zz * 16:(zz + 1) * 16]
    half = pl.ds(core * 4, 4)
    lanes = pl.ds(pl.multiple_of(q * B, B), B)
    x_own = pltpu.make_async_copy(xs.at[half], xt.at[half, :, lanes], loc.at[3])
    x_own.start()

    upper = lax.broadcasted_iota(jnp.int32, (B, B), 1) >= lax.broadcasted_iota(
        jnp.int32, (B, B), 0
    )
    for k in range(3):
        def build(n, before, k=k):
            row = taps[k:k + 1, pl.ds(pl.multiple_of(n * B, B), B)]
            turned = pltpu.roll(
                jnp.broadcast_to(row, (B, B)), 0, 1, stride=1, stride_axis=0
            )
            block = jnp.where(upper, turned, before)
            hank[lax.rem(n, 8), k * B:(k + 1) * B,
                 pl.ds(pl.multiple_of(lax.div(n, 8) * B, B), B)] = block.astype(BF16)
            return turned

        lax.fori_loop(0, 64, build, jnp.zeros((B, B), F32), unroll=2)

    def sub(slot, s):
        return gl.at[slot, core, pl.ds(s * 4, 4)]

    def ring_send(step, s, way):
        here = -step % 8 if way == 0 else step
        there = (-step - 1) % 8 if way == 0 else step + 1
        return remote(
            sub(here, s), sub(there, s),
            gr_s.at[way, step, s], gr_r.at[way, step, s], up if way == 0 else down,
        )

    def hand_over(slot, s):
        return remote(sub(slot, s), sub(slot, s), gs_s.at[slot, s], gs_r.at[slot, s], sib)

    def handed(slot, s):
        other = gl.at[slot, 1 - core, pl.ds(s * 4, 4)]
        return remote(other, other, gs_s.at[slot, s], gs_r.at[slot, s], sib)

    for c in a2a:
        c.wait_recv()
    for s in range(2):
        for way in range(2):
            go(ring_send(0, s, way))
    for s in range(2):
        go(hand_over(0, s))

    x_sends = []
    for r in range(1, 8):
        x_sends.append(
            remote(xs.at[half], xt.at[half, :, lanes], xa_s.at[r], xa_r.at[r], plane(0, r))
        )
        go(x_sends[-1])

    first = [True]

    def conv(o):
        slot = o % 8
        for s in range(2):
            handed(slot, s).wait_recv()
        buf = g2.at[0]
        for m in range(8):
            for h in range(2):
                piece = gl[slot, h, m]
                buf[m * B + h * 64:m * B + h * 64 + 64, 0:B] = piece
                if m > 0:
                    buf[(m - 1) * B + h * 64:(m - 1) * B + h * 64 + 64, B:2 * B] = piece
        wrap = jnp.where(lax.rem(z + o + 8, 8) < z, 1, 0)
        for p in range(4):
            depth = B * (8 - 2 * p)
            start = pl.multiple_of(wrap * B + 2 * p * B, B)
            term = jnp.dot(
                hank[slot, :, 0:depth], buf[pl.ds(start, depth), :],
                preferred_element_type=F32,
            )
            if first[0]:
                acc[p] = term
            else:
                acc[p] += term
        first[0] = False

    conv(0)
    for step in range(1, 4):
        for s in range(2):
            for way in range(2):
                ring_send(step - 1, s, way).wait_recv()
                slot = -step % 8 if way == 0 else step
                if step < 3 or s == way:
                    go(ring_send(step, s, way))
                go(hand_over(slot, s))
        if step == 3:
            x_own.wait()
            for c in x_sends:
                c.wait_recv()
            x_hand = remote(xt.at[half], xt.at[half], xs_s, xs_r, sib)
            go(x_hand)
        conv(step)
        conv(-step)
    for way in range(2):
        ring_send(3, way, way).wait_recv()
        go(hand_over(4, way))
    conv(4)

    for p in range(4):
        for e in range(2):
            for k in range(3):
                corr[(2 * p + e) * B:(2 * p + e + 1) * B, k * B:(k + 1) * B] = acc[
                    p, k * B:(k + 1) * B, e * B:(e + 1) * B
                ].astype(BF16)

    half_o = pl.ds((1 - core) * 4, 4)
    remote(xt.at[half_o], xt.at[half_o], xs_s, xs_r, sib).wait_recv()
    for zz in range(8):
        part = jnp.dot(xt[zz], corr[...], preferred_element_type=F32).astype(BF16)
        for k in range(3):
            pgb[zz, k] = part[:, k * B:(k + 1) * B]

    def at(o):
        return lax.rem(z + o + 8, 8)

    def sum_send(step, k, way):
        src = pgb.at[at(4 if way == 0 else -3), k] if step == 0 else pgs.at[way, step - 1, k]
        return remote(
            src, pgr.at[way, step, k], pr_s.at[way, step, k], pr_r.at[way, step, k],
            up if way == 0 else down,
        )

    def sum_step(step):
        for k in range(3):
            for way in range(2):
                if way == 1 and step == 3:
                    continue
                sum_send(step - 1, k, way).wait_recv()
                o = 4 - step if way == 0 else step - 3
                pgs[way, step - 1, k] = (
                    pgr[way, step - 1, k].astype(F32) + pgb[at(o), k].astype(F32)
                ).astype(BF16)
                go(sum_send(step, k, way))

    for k in range(3):
        for way in range(2):
            go(sum_send(0, k, way))

    for p in p_copies:
        p.wait()

    def tile(x_to, of_core):
        cols = pl.ds(pl.multiple_of(x_to * 512 + of_core * 256, 256), 256)
        return lax.dot_general(
            corr[...], pn[cols, :], (((1,), (1,)), ((), ())), preferred_element_type=F32
        )

    swaps = []
    for x_to in range(2):
        igs[x_to] = tile(x_to, 1 - core).astype(BF16).reshape(8, B, 256)
        swaps.append(remote(igs.at[x_to], igr.at[x_to], is_s.at[x_to], is_r.at[x_to], sib))
        go(swaps[-1])
    sum_step(1)
    for x_to in range(2):
        igo[x_to] = tile(x_to, core).reshape(8, B, 256)
    sum_step(2)
    for x_to in range(2):
        swaps[x_to].wait_recv()
        igc[x_to] = (igo[x_to] + igr[x_to].astype(F32)).astype(BF16)
    ig_sends = []
    for r in range(1, 16):
        dx, dq = r // 8, r % 8
        ig_sends.append(
            remote(
                igc.at[lax.rem(xh + dx, 2), lax.rem(q + dq, 8)], igd.at[r],
                id_s.at[r], id_r.at[r], plane(dx, dq),
            )
        )
        go(ig_sends[-1])
    sum_step(3)

    scale = 8192.0 ** -0.5
    for k in range(3):
        sum_send(2, k, 1).wait_recv()
        sum_send(3, k, 0).wait_recv()
        total = (
            pgr[0, 3, k].astype(F32) + pgr[1, 2, k].astype(F32) + pgb[z, k].astype(F32)
        ) * scale
        pga[:, k] = total.astype(BF16).reshape(8, 16, B)
    pg_sends = []
    for r in range(1, 8):
        pg_sends.append(
            remote(
                pga.at[lax.rem(q + r, 8)], pgo.at[q], pa_s.at[r], pa_r.at[r], plane(0, r)
            )
        )
        go(pg_sends[-1])
    pgo[q] = pga[q]

    for c in ig_sends:
        c.wait_recv()
    total = igc[xh, q].astype(F32)
    for r in range(1, 16):
        total = total + igd[r].astype(F32)
    ig_ref[...] = total.astype(BF16)

    for c in pg_sends:
        c.wait_recv()
    for s in range(8):
        pg_ref[:, :, s * B:(s + 1) * B] = pgo[s]
    for c in sent:
        c.wait_send()


def per_device(inputs, cotangent, filters, projections):
    vmem = pl.BlockSpec(memory_space=pltpu.VMEM)
    dma = pltpu.SemaphoreType.DMA
    return pl.pallas_call(
        kernel,
        out_shape=(
            jax.ShapeDtypeStruct((B, 256), BF16),
            jax.ShapeDtypeStruct((3, 16, 1024), BF16),
        ),
        in_specs=[vmem, vmem, vmem, pl.BlockSpec(memory_space=pl.ANY)],
        out_specs=(vmem, vmem),
        scratch_shapes=[
            pltpu.VMEM((8, 8192), F32),
            pltpu.VMEM((8, 384, 1024), BF16),
            pltpu.VMEM((8, 2, 8, 64, B), BF16),
            pltpu.VMEM((1, 1152, 256), BF16),
            pltpu.VMEM((4, 384, 256), F32),
            pltpu.VMEM((1024, 384), BF16),
            pltpu.VMEM((8, B, B), BF16),
            pltpu.VMEM((8, B, 1024), BF16),
            pltpu.VMEM((1024, 384), BF16),
            pltpu.VMEM((8, 3, B, B), BF16),
            pltpu.VMEM((2, 4, 3, B, B), BF16),
            pltpu.VMEM((2, 3, 3, B, B), BF16),
            pltpu.VMEM((8, 3, 16, B), BF16),
            pltpu.VMEM((8, 3, 16, B), BF16),
            pltpu.VMEM((2, 8, B, 256), BF16),
            pltpu.VMEM((2, 8, B, 256), BF16),
            pltpu.VMEM((2, 8, B, 256), F32),
            pltpu.VMEM((2, 8, B, 256), BF16),
            pltpu.VMEM((16, B, 256), BF16),
            dma((8,)), dma((8,)),
            dma((2, 4, 2)), dma((2, 4, 2)),
            dma((8, 2)), dma((8, 2)),
            dma((8,)), dma((8,)),
            dma, dma,
            dma((4,)),
            dma((2, 4, 3)), dma((2, 4, 3)),
            dma((8,)), dma((8,)),
            dma((2,)), dma((2,)),
            dma((16,)), dma((16,)),
        ],
        compiler_params=pltpu.CompilerParams(
            collective_id=0, has_side_effects=True, vmem_limit_bytes=48 * 1024 * 1024
        ),
        cost_estimate=pl.CostEstimate(
            flops=6_000_000_000, bytes_accessed=2_000_000, transcendentals=0
        ),
    )(inputs, cotangent, filters, projections)


def solution(mesh):
    placed = (P("seq", None), P("seq", None), P(), P("filt", None, None))
    return jax.shard_map(
        per_device,
        mesh=mesh,
        in_specs=placed,
        out_specs=(P("seq", "filt"), P("filt", "seq", None)),
        check_vma=False,
    )
```

time: 938 us -> 69.7 us (0.07)
  the two profiles are of different devices: /device:TPU:4 before, /device:TPU:1 now
where the time goes in v1:
time: 69.7 us; the launch traced here: 69.2 us
  Pallas kernels  64.4 us (92%)
  local copies, waits for them, and re-layouts  4.11 us (6%)
    pallas_call x1, Pallas kernels, per_device(): pl.pallas_call(kernel, out_shape=(jax.ShapeDtypeStruct((B, 256), BF16), j...  64.4 us
    unnamed x8, local copies, waits for them, and re-layouts  4.11 us

profile of v1, /device:TPU:1, one launch (start us, length us, event | category | flops | bytes accessed | tf_op | source)
XLA Modules:
  0.0 69.2 jit_solution(1550140950927022256)
XLA Ops:
  0.6 0.0 copy-start
  0.6 0.9 %copy-done = bf16[128,1024]{1,0:T(8,128)(2,1)S(1)} copy-done((bf16[128,1024]{1,0:T(8,128)(2,1)S(1)}, bf16[128,1024]{1,0:T(8,128)(2,1)}, u32[]{:S(2)}) %copy-start) | copy-done | bytes 262168
  1.6 0.0 copy-start.1
  1.6 0.9 %copy-done.1 = bf16[128,1024]{1,0:T(8,128)(2,1)S(1)} copy-done((bf16[128,1024]{1,0:T(8,128)(2,1)S(1)}, bf16[128,1024]{1,0:T(8,128)(2,1)}, u32[]{:S(2)}) %copy-start.1) | copy-done | bytes 262168
  2.5 0.0 copy-start.2
  2.5 0.9 %copy-done.2 = bf16[12,8192]{1,0:T(8,128)(2,1)S(1)} copy-done((bf16[12,8192]{1,0:T(8,128)(2,1)S(1)}, bf16[12,8192]{1,0:T(8,128)(2,1)}, u32[]{:S(2)}) %copy-start.2) | copy-done | bytes 196632
  3.5 64.4 %shard_map.59 = (bf16[128,256]{1,0:T(8,128)(2,1)S(1)}, bf16[3,16,1024]{2,1,0:T(8,128)(2,1)S(1)}) custom-call(bf16[128,1024]{1,0:T(8,128)(2,1)S(1)} %copy-done, bf16[128,1024]{1,0:T(8,128)(2,1)S(1)} %copy-done.1, bf16[12,8192]{1,0:T(8,128)(2,1)S(1)} %copy-done.2, bf16[3,1024,1024]{2,1,0:T(8,128)(2,1)} %p_ref.1), custom_call_target="tpu_custom_call" | custom-call | flops 6000000000 | bytes 2000000 | tf_op jit(solution)/shard_map/pallas_call | solution.py:298
  67.9 0.6 copy.8
  68.5 0.6 copy.9
Async XLA Ops:
  0.6 1.0 %copy-start = (bf16[128,1024]{1,0:T(8,128)(2,1)S(1)}, bf16[128,1024]{1,0:T(8,128)(2,1)}, u32[]{:S(2)}) copy-start(bf16[128,1024]{1,0:T(8,128)(2,1)} %x_ref.1) | copy-start | bytes 786436
  1.6 0.9 %copy-start.1 = (bf16[128,1024]{1,0:T(8,128)(2,1)S(1)}, bf16[128,1024]{1,0:T(8,128)(2,1)}, u32[]{:S(2)}) copy-start(bf16[128,1024]{1,0:T(8,128)(2,1)} %g_ref.1) | copy-start | bytes 786436
  2.5 0.9 %copy-start.2 = (bf16[12,8192]{1,0:T(8,128)(2,1)S(1)}, bf16[12,8192]{1,0:T(8,128)(2,1)}, u32[]{:S(2)}) copy-start(bf16[12,8192]{1,0:T(8,128)(2,1)} %f_ref.1) | copy-start | bytes 589828

commit v2 on v1

--- a/solution.py
+++ b/solution.py
@@ -16,7 +16,7 @@
 
 def kernel(
     x_ref, g_ref, f_ref, p_ref, ig_ref, pg_ref,
-    taps, hank, gl, g2, acc, corr, xs, xt, pn, pgb, pgr, pgs, pga, pgo,
+    taps, fv, gv, xv, hank, gl, g2, acc, corr, xs, xt, pn, pgb, pgr, pgs, pga, pgo,
     igs, igr, igo, igc, igd,
     ga_s, ga_r, gr_s, gr_r, gs_s, gs_r, xa_s, xa_r, xs_s, xs_r, loc,
     pr_s, pr_r, pa_s, pa_r, is_s, is_r, id_s, id_r,
@@ -49,25 +49,52 @@
     for to in partners:
         pl.semaphore_signal(barrier, inc=1, device_id=to, device_id_type=MESH)
 
+    rows = pl.ds(pl.multiple_of(core * 64, 64), 64)
+    lanes = pl.ds(pl.multiple_of(q * B, B), B)
+    f_in = pltpu.make_async_copy(f_ref, fv, loc.at[4])
+    g_in = pltpu.make_async_copy(g_ref.at[rows], gv, loc.at[5])
+    g_own = pltpu.make_async_copy(g_ref.at[rows, lanes], gl.at[0, core, q], loc.at[6])
+    x_in = pltpu.make_async_copy(x_ref, xv, loc.at[7])
     p_copies = [
-        pltpu.make_async_copy(
-            p_ref.at[k, :, pl.ds(pl.multiple_of(q * B, B), B)],
-            pn.at[:, pl.ds(k * B, B)],
-            loc.at[k],
-        )
+        pltpu.make_async_copy(p_ref.at[k, :, lanes], pn.at[:, pl.ds(k * B, B)], loc.at[k])
         for k in range(3)
     ]
-    for c in p_copies:
+    for c in [f_in, g_in, g_own, x_in] + p_copies:
         c.start()
+    f_in.wait()
     pick = jnp.where(
         lax.broadcasted_iota(jnp.int32, (8, 12), 1)
         == lax.broadcasted_iota(jnp.int32, (8, 12), 0) + 3 * filt,
         1.0, 0.0,
     ).astype(BF16)
-    taps[...] = jnp.dot(pick, f_ref[...], preferred_element_type=F32)
-    g2[...] = jnp.zeros_like(g2)
-    rows = pl.ds(pl.multiple_of(core * 64, 64), 64)
-    gl[0, core, q] = g_ref[rows, pl.ds(pl.multiple_of(q * B, B), B)]
+    taps[:, 0:B] = jnp.zeros((8, B), F32)
+    taps[:, B:] = jnp.dot(pick, fv[...], preferred_element_type=F32)
+    g2[0, 1024:1152, 0:B] = jnp.zeros((B, B), BF16)
+    g2[0, 896:1152, B:2 * B] = jnp.zeros((2 * B, B), BF16)
+
+    def build(j, carry):
+        for i in range(8):
+            upper = lax.broadcasted_iota(jnp.int32, (16, B), 1) >= (
+                lax.broadcasted_iota(jnp.int32, (16, B), 0) + 16 * i
+            )
+            for k in range(3):
+                before = None
+                for d in range(-1, 8):
+                    row = taps[k:k + 1, pl.ds(pl.multiple_of((8 * j + d + 1) * B, B), B)]
+                    turned = pltpu.roll(
+                        jnp.broadcast_to(row, (16, B)), 16 * i, 1, stride=1, stride_axis=0
+                    )
+                    if d >= 0:
+                        hank[d, k * B + 16 * i:k * B + 16 * i + 16,
+                             pl.ds(pl.multiple_of(j * B, B), B)] = jnp.where(
+                                 upper, turned, before
+                             ).astype(BF16)
+                    before = turned
+        return carry
+
+    lax.fori_loop(0, 4, build, 0)
+    g_in.wait()
+    g_own.wait()
 
     pl.semaphore_wait(barrier, len(partners))
 
@@ -75,37 +102,22 @@
     for r in range(1, 8):
         col = pl.ds(pl.multiple_of(lax.rem(q + r, 8) * B, B), B)
         a2a.append(
-            remote(g_ref.at[rows, col], gl.at[0, core, q], ga_s.at[r], ga_r.at[r], plane(0, r))
+            remote(gv.at[:, col], gl.at[0, core, q], ga_s.at[r], ga_r.at[r], plane(0, r))
         )
         go(a2a[-1])
-
+    lax.fori_loop(4, 8, build, 0)
+
+    x_in.wait()
     for t in range(8):
-        flip = x_ref[:, t * B:(t + 1) * B].T
+        flip = xv[:, t * B:(t + 1) * B].T
         for zz in range(8):
             xs[zz, t * 16:(t + 1) * 16, :] = flip[zz * 16:(zz + 1) * 16]
     half = pl.ds(core * 4, 4)
-    lanes = pl.ds(pl.multiple_of(q * B, B), B)
     x_own = pltpu.make_async_copy(xs.at[half], xt.at[half, :, lanes], loc.at[3])
     x_own.start()
 
-    upper = lax.broadcasted_iota(jnp.int32, (B, B), 1) >= lax.broadcasted_iota(
-        jnp.int32, (B, B), 0
-    )
-    for k in range(3):
-        def build(n, before, k=k):
-            row = taps[k:k + 1, pl.ds(pl.multiple_of(n * B, B), B)]
-            turned = pltpu.roll(
-                jnp.broadcast_to(row, (B, B)), 0, 1, stride=1, stride_axis=0
-            )
-            block = jnp.where(upper, turned, before)
-            hank[lax.rem(n, 8), k * B:(k + 1) * B,
-                 pl.ds(pl.multiple_of(lax.div(n, 8) * B, B), B)] = block.astype(BF16)
-            return turned
-
-        lax.fori_loop(0, 64, build, jnp.zeros((B, B), F32), unroll=2)
-
     def sub(slot, s):
-        return gl.at[slot, core, pl.ds(s * 4, 4)]
+        return gl.at[slot, core, pl.ds(s * 2, 2)]
 
     def ring_send(step, s, way):
         here = -step % 8 if way == 0 else step
@@ -115,20 +127,20 @@
             gr_s.at[way, step, s], gr_r.at[way, step, s], up if way == 0 else down,
         )
 
-    def hand_over(slot, s):
-        return remote(sub(slot, s), sub(slot, s), gs_s.at[slot, s], gs_r.at[slot, s], sib)
-
-    def handed(slot, s):
-        other = gl.at[slot, 1 - core, pl.ds(s * 4, 4)]
-        return remote(other, other, gs_s.at[slot, s], gs_r.at[slot, s], sib)
+    def hand_over(slot):
+        mine = gl.at[slot, core]
+        return remote(mine, mine, gs_s.at[slot], gs_r.at[slot], sib)
+
+    def handed(slot):
+        other = gl.at[slot, 1 - core]
+        return remote(other, other, gs_s.at[slot], gs_r.at[slot], sib)
 
     for c in a2a:
         c.wait_recv()
-    for s in range(2):
+    for s in range(4):
         for way in range(2):
             go(ring_send(0, s, way))
-    for s in range(2):
-        go(hand_over(0, s))
+    go(hand_over(0))
 
     x_sends = []
     for r in range(1, 8):
@@ -137,12 +149,9 @@
         )
         go(x_sends[-1])
 
-    first = [True]
-
     def conv(o):
         slot = o % 8
-        for s in range(2):
-            handed(slot, s).wait_recv()
+        handed(slot).wait_recv()
         buf = g2.at[0]
         for m in range(8):
             for h in range(2):
@@ -158,48 +167,45 @@
                 hank[slot, :, 0:depth], buf[pl.ds(start, depth), :],
                 preferred_element_type=F32,
             )
-            if first[0]:
+            if o == 0:
                 acc[p] = term
+            elif o != 4:
+                acc[p] += term
             else:
-                acc[p] += term
-        first[0] = False
+                done = (acc[p] + term).astype(BF16)
+                for e in range(2):
+                    for k in range(3):
+                        corr[(2 * p + e) * B:(2 * p + e + 1) * B, k * B:(k + 1) * B] = done[
+                            k * B:(k + 1) * B, e * B:(e + 1) * B
+                        ]
 
     conv(0)
     for step in range(1, 4):
-        for s in range(2):
+        for s in range(4):
             for way in range(2):
                 ring_send(step - 1, s, way).wait_recv()
-                slot = -step % 8 if way == 0 else step
-                if step < 3 or s == way:
+                if step < 3 or s // 2 == way:
                     go(ring_send(step, s, way))
-                go(hand_over(slot, s))
+        go(hand_over(-step % 8))
+        go(hand_over(step))
+        if step > 1:
+            conv(step - 1)
+            conv(1 - step)
         if step == 3:
             x_own.wait()
             for c in x_sends:
                 c.wait_recv()
             x_hand = remote(xt.at[half], xt.at[half], xs_s, xs_r, sib)
             go(x_hand)
-        conv(step)
-        conv(-step)
-    for way in range(2):
-        ring_send(3, way, way).wait_recv()
-        go(hand_over(4, way))
+    for s in range(4):
+        ring_send(3, s, s // 2).wait_recv()
+    go(hand_over(4))
+    conv(3)
+    conv(-3)
     conv(4)
-
-    for p in range(4):
-        for e in range(2):
-            for k in range(3):
-                corr[(2 * p + e) * B:(2 * p + e + 1) * B, k * B:(k + 1) * B] = acc[
-                    p, k * B:(k + 1) * B, e * B:(e + 1) * B
-                ].astype(BF16)
 
     half_o = pl.ds((1 - core) * 4, 4)
     remote(xt.at[half_o], xt.at[half_o], xs_s, xs_r, sib).wait_recv()
-    for zz in range(8):
-        part = jnp.dot(xt[zz], corr[...], preferred_element_type=F32).astype(BF16)
-        for k in range(3):
-            pgb[zz, k] = part[:, k * B:(k + 1) * B]
-
     def at(o):
         return lax.rem(z + o + 8, 8)
 
@@ -222,9 +228,14 @@
                 ).astype(BF16)
                 go(sum_send(step, k, way))
 
-    for k in range(3):
-        for way in range(2):
-            go(sum_send(0, k, way))
+    for o in (4, -3, 3, -2, 2, -1, 1, 0):
+        part = jnp.dot(xt[at(o)], corr[...], preferred_element_type=F32).astype(BF16)
+        for k in range(3):
+            pgb[at(o), k] = part[:, k * B:(k + 1) * B]
+        if o == -3:
+            for k in range(3):
+                for way in range(2):
+                    go(sum_send(0, k, way))
 
     for p in p_copies:
         p.wait()
@@ -301,10 +312,13 @@
             jax.ShapeDtypeStruct((B, 256), BF16),
             jax.ShapeDtypeStruct((3, 16, 1024), BF16),
         ),
-        in_specs=[vmem, vmem, vmem, pl.BlockSpec(memory_space=pl.ANY)],
+        in_specs=[pl.BlockSpec(memory_space=pl.ANY)] * 4,
         out_specs=(vmem, vmem),
         scratch_shapes=[
-            pltpu.VMEM((8, 8192), F32),
+            pltpu.VMEM((8, 8192 + B), F32),
+            pltpu.VMEM((12, 8192), BF16),
+            pltpu.VMEM((64, 1024), BF16),
+            pltpu.VMEM((B, 1024), BF16),
             pltpu.VMEM((8, 384, 1024), BF16),
             pltpu.VMEM((8, 2, 8, 64, B), BF16),
             pltpu.VMEM((1, 1152, 256), BF16),
@@ -324,18 +338,18 @@
             pltpu.VMEM((2, 8, B, 256), BF16),
             pltpu.VMEM((16, B, 256), BF16),
             dma((8,)), dma((8,)),
-            dma((2, 4, 2)), dma((2, 4, 2)),
-            dma((8, 2)), dma((8, 2)),
+            dma((2, 4, 4)), dma((2, 4, 4)),
+            dma((8,)), dma((8,)),
             dma((8,)), dma((8,)),
             dma, dma,
-            dma((4,)),
+            dma((8,)),
             dma((2, 4, 3)), dma((2, 4, 3)),
             dma((8,)), dma((8,)),
             dma((2,)), dma((2,)),
             dma((16,)), dma((16,)),
         ],
         compiler_params=pltpu.CompilerParams(
-            collective_id=0, has_side_effects=True, vmem_limit_bytes=48 * 1024 * 1024
+            collective_id=0, has_side_effects=True, vmem_limit_bytes=58 * 1024 * 1024
         ),
         cost_estimate=pl.CostEstimate(
             flops=6_000_000_000, bytes_accessed=2_000_000, transcendentals=0

time: 69.7 us -> 60.4 us (0.87)
  Pallas kernels: 64.4 us -> 56.6 us
  local copies, waits for them, and re-layouts: 4.11 us -> 3.01 us
    pallas_call x1, Pallas kernels: 64.4 us -> 56.6 us  [per_device(): pl.pallas_call(kernel, out_shape=(jax.ShapeDtypeStruct((B, 256), BF16), j...]
    unnamed x8 -> x2, local copies, waits for them, and re-layouts: 4.11 us -> 3.01 us
where the time goes in v2:
time: 60.4 us; the launch traced here: 60.2 us
  Pallas kernels  56.6 us (94%)
  local copies, waits for them, and re-layouts  3.01 us (5%)
  between operations  0.64 us (1%)
    pallas_call x1, Pallas kernels, per_device(): pl.pallas_call(kernel, out_shape=(jax.ShapeDtypeStruct((B, 256), BF16), j...  56.6 us
    unnamed x2, local copies, waits for them, and re-layouts  3.01 us

profile of v2, /device:TPU:1, one launch (start us, length us, event | category | flops | bytes accessed | tf_op | source)
XLA Modules:
  0.0 60.2 jit_solution(16762875053460633810)
XLA Ops:
  0.6 56.6 %shard_map.59 = (bf16[128,256]{1,0:T(8,128)(2,1)}, bf16[3,16,1024]{2,1,0:T(8,128)(2,1)}) custom-call(bf16[128,1024]{1,0:T(8,128)(2,1)} %x_ref.1, bf16[128,1024]{1,0:T(8,128)(2,1)} %g_ref.1, bf16[12,8192]{1,0:T(8,128)(2,1)} %f_ref.1, bf16[3,1024,1024]{2,1,0:T(8,128)(2,1)} %p_ref.1), custom_call_target="tpu_custom_call" | custom-call | flops 6000000000 | bytes 2000000 | tf_op jit(solution)/shard_map/pallas_call | solution.py:309
  57.2 1.5 %copy.8 = bf16[128,256]{1,0:T(8,128)(2,1)} copy(bf16[128,256]{1,0:T(8,128)(2,1)} %get-tuple-element.4) | data formatting | bytes 131072
  58.7 1.5 %copy.9 = bf16[3,16,1024]{2,1,0:T(8,128)(2,1)} copy(bf16[3,16,1024]{2,1,0:T(8,128)(2,1)} %get-tuple-element.5) | data formatting | bytes 196608

commit v3 on v2

--- a/solution.py
+++ b/solution.py
@@ -16,9 +16,9 @@
 
 def kernel(
     x_ref, g_ref, f_ref, p_ref, ig_ref, pg_ref,
-    taps, fv, gv, xv, hank, gl, g2, acc, corr, xs, xt, pn, pgb, pgr, pgs, pga, pgo,
+    taps, fv, xv, hank, gl, g2, acc, corr, xs, xt, pn, pgb, pgr, pgs, pga, pgo, pgp,
     igs, igr, igo, igc, igd,
-    ga_s, ga_r, gr_s, gr_r, gs_s, gs_r, xa_s, xa_r, xs_s, xs_r, loc,
+    ga_s, ga_r, gr_s, gr_r, gs_s, gs_r, ge_s, ge_r, xa_s, xa_r, xs_s, xs_r, loc,
     pr_s, pr_r, pa_s, pa_r, is_s, is_r, id_s, id_r,
 ):
     seq = lax.axis_index("seq")
@@ -44,22 +44,28 @@
         copy.start()
         sent.append(copy)
 
+    def near(dz, dq):
+        return (lax.rem(q + dq, 8) * 8 + lax.rem(z + dz + 8, 8), filt)
+
     barrier = pltpu.get_barrier_semaphore()
-    partners = [sib, up, down] + [plane(r // 8, r % 8) for r in range(1, 16)]
+    partners = (
+        [sib]
+        + [plane(r // 8, r % 8) for r in range(1, 16)]
+        + [near(dz, r) for dz in (1, -1) for r in range(8)]
+    )
     for to in partners:
         pl.semaphore_signal(barrier, inc=1, device_id=to, device_id_type=MESH)
 
     rows = pl.ds(pl.multiple_of(core * 64, 64), 64)
     lanes = pl.ds(pl.multiple_of(q * B, B), B)
     f_in = pltpu.make_async_copy(f_ref, fv, loc.at[4])
-    g_in = pltpu.make_async_copy(g_ref.at[rows], gv, loc.at[5])
     g_own = pltpu.make_async_copy(g_ref.at[rows, lanes], gl.at[0, core, q], loc.at[6])
     x_in = pltpu.make_async_copy(x_ref, xv, loc.at[7])
     p_copies = [
         pltpu.make_async_copy(p_ref.at[k, :, lanes], pn.at[:, pl.ds(k * B, B)], loc.at[k])
         for k in range(3)
     ]
-    for c in [f_in, g_in, g_own, x_in] + p_copies:
+    for c in [f_in, g_own, x_in] + p_copies:
         c.start()
     f_in.wait()
     pick = jnp.where(
@@ -93,18 +99,23 @@
         return carry
 
     lax.fori_loop(0, 4, build, 0)
-    g_in.wait()
     g_own.wait()
 
     pl.semaphore_wait(barrier, len(partners))
 
-    a2a = []
-    for r in range(1, 8):
+    pieces = []
+    for r in range(8):
         col = pl.ds(pl.multiple_of(lax.rem(q + r, 8) * B, B), B)
-        a2a.append(
-            remote(gv.at[:, col], gl.at[0, core, q], ga_s.at[r], ga_r.at[r], plane(0, r))
-        )
-        go(a2a[-1])
+        for d, dz in ((1, 1), (2, -1), (0, 0)):
+            if r == 0 and dz == 0:
+                continue
+            c = remote(
+                g_ref.at[rows, col], gl.at[-dz % 8, core, q], ga_s.at[d, r],
+                ga_r.at[d, r if dz == 0 else q], near(dz, r),
+            )
+            go(c)
+            if dz == 0:
+                pieces.append(c)
     lax.fori_loop(4, 8, build, 0)
 
     x_in.wait()
@@ -135,12 +146,20 @@
         other = gl.at[slot, 1 - core]
         return remote(other, other, gs_s.at[slot], gs_r.at[slot], sib)
 
-    for c in a2a:
+    def landed(d, m):
+        here = gl.at[-1 % 8 if d == 1 else 1, core, m]
+        return remote(here, here, ga_s.at[d, 0], ga_r.at[d, m], up)
+
+    for c in pieces:
         c.wait_recv()
+    go(hand_over(0))
     for s in range(4):
         for way in range(2):
-            go(ring_send(0, s, way))
-    go(hand_over(0))
+            landed(way + 1, 2 * s).wait_recv()
+            landed(way + 1, 2 * s + 1).wait_recv()
+            go(ring_send(1, s, way))
+    go(hand_over(-1 % 8))
+    go(hand_over(1))
 
     x_sends = []
     for r in range(1, 8):
@@ -151,7 +170,12 @@
 
     def conv(o):
         slot = o % 8
-        handed(slot).wait_recv()
+        if o == 4:
+            for s in range(4):
+                other = gl.at[4, 1 - core, pl.ds(s * 2, 2)]
+                remote(other, other, ge_s.at[s], ge_r.at[s], sib).wait_recv()
+        else:
+            handed(slot).wait_recv()
         buf = g2.at[0]
         for m in range(8):
             for h in range(2):
@@ -180,7 +204,7 @@
                         ]
 
     conv(0)
-    for step in range(1, 4):
+    for step in range(2, 4):
         for s in range(4):
             for way in range(2):
                 ring_send(step - 1, s, way).wait_recv()
@@ -188,26 +212,56 @@
                     go(ring_send(step, s, way))
         go(hand_over(-step % 8))
         go(hand_over(step))
-        if step > 1:
-            conv(step - 1)
-            conv(1 - step)
+        conv(step - 1)
+        conv(1 - step)
         if step == 3:
             x_own.wait()
             for c in x_sends:
                 c.wait_recv()
             x_hand = remote(xt.at[half], xt.at[half], xs_s, xs_r, sib)
             go(x_hand)
+    conv(3)
     for s in range(4):
         ring_send(3, s, s // 2).wait_recv()
-    go(hand_over(4))
-    conv(3)
+        mine = sub(4, s)
+        go(remote(mine, mine, ge_s.at[s], ge_r.at[s], sib))
     conv(-3)
     conv(4)
 
+    for p in p_copies:
+        p.wait()
+
+    def tile(x_to, of_core, upper_half):
+        cols = pl.ds(pl.multiple_of(x_to * 512 + of_core * 256, 256), 256)
+        return lax.dot_general(
+            corr[upper_half * 512:upper_half * 512 + 512], pn[cols, :],
+            (((1,), (1,)), ((), ())), preferred_element_type=F32,
+        ).reshape(4, B, 256)
+
+    quarters = [(x_to, u) for u in range(2) for x_to in range(2)]
+    swaps = []
+    for n, (x_to, u) in enumerate(quarters):
+        part = pl.ds(u * 4, 4)
+        igs[x_to, part] = tile(x_to, 1 - core, u).astype(BF16)
+        swaps.append(
+            remote(igs.at[x_to, part], igr.at[x_to, part], is_s.at[n], is_r.at[n], sib)
+        )
+        go(swaps[-1])
+
     half_o = pl.ds((1 - core) * 4, 4)
     remote(xt.at[half_o], xt.at[half_o], xs_s, xs_r, sib).wait_recv()
+
     def at(o):
         return lax.rem(z + o + 8, 8)
+
+    def products(*offsets):
+        for o in offsets:
+            part = jnp.dot(xt[at(o)], corr[...], preferred_element_type=F32).astype(BF16)
+            for k in range(3):
+                if o == 0:
+                    pgo[:, k] = part[:, k * B:(k + 1) * B].reshape(8, 16, B)
+                else:
+                    pgb[at(o), k] = part[:, k * B:(k + 1) * B]
 
     def sum_send(step, k, way):
         src = pgb.at[at(4 if way == 0 else -3), k] if step == 0 else pgs.at[way, step - 1, k]
@@ -216,49 +270,39 @@
             up if way == 0 else down,
         )
 
-    def sum_step(step):
+    def sum_step(step, way):
+        last = step == (3 if way == 0 else 2)
+        o = 4 - step if way == 0 else step - 3
         for k in range(3):
-            for way in range(2):
-                if way == 1 and step == 3:
-                    continue
-                sum_send(step - 1, k, way).wait_recv()
-                o = 4 - step if way == 0 else step - 3
-                pgs[way, step - 1, k] = (
-                    pgr[way, step - 1, k].astype(F32) + pgb[at(o), k].astype(F32)
-                ).astype(BF16)
+            sum_send(step - 1, k, way).wait_recv()
+            total = (
+                pgr[way, step - 1, k].astype(F32) + pgb[at(o), k].astype(F32)
+            ).astype(BF16)
+            if last:
+                pga[way, :, k] = total.reshape(8, 16, B)
+            else:
+                pgs[way, step - 1, k] = total
                 go(sum_send(step, k, way))
-
-    for o in (4, -3, 3, -2, 2, -1, 1, 0):
-        part = jnp.dot(xt[at(o)], corr[...], preferred_element_type=F32).astype(BF16)
-        for k in range(3):
-            pgb[at(o), k] = part[:, k * B:(k + 1) * B]
-        if o == -3:
-            for k in range(3):
-                for way in range(2):
-                    go(sum_send(0, k, way))
-
-    for p in p_copies:
-        p.wait()
-
-    def tile(x_to, of_core):
-        cols = pl.ds(pl.multiple_of(x_to * 512 + of_core * 256, 256), 256)
-        return lax.dot_general(
-            corr[...], pn[cols, :], (((1,), (1,)), ((), ())), preferred_element_type=F32
-        )
-
-    swaps = []
-    for x_to in range(2):
-        igs[x_to] = tile(x_to, 1 - core).astype(BF16).reshape(8, B, 256)
-        swaps.append(remote(igs.at[x_to], igr.at[x_to], is_s.at[x_to], is_r.at[x_to], sib))
-        go(swaps[-1])
-    sum_step(1)
-    for x_to in range(2):
-        igo[x_to] = tile(x_to, core).reshape(8, B, 256)
-    sum_step(2)
-    for x_to in range(2):
-        swaps[x_to].wait_recv()
-        igc[x_to] = (igo[x_to] + igr[x_to].astype(F32)).astype(BF16)
+        if last:
+            for r in range(8):
+                go(remote(
+                    pga.at[way, lax.rem(q + r, 8)], pgp.at[way + 1, q],
+                    pa_s.at[way + 1, r], pa_r.at[way + 1, q], near(1 if way == 0 else -1, r),
+                ))
+
+    products(4, -3)
+    for k in range(3):
+        for way in range(2):
+            go(sum_send(0, k, way))
+    for n, (x_to, u) in enumerate(quarters):
+        igo[x_to, u * 4:u * 4 + 4] = tile(x_to, core, u)
+    products(3, -2)
+
     ig_sends = []
+    for n, (x_to, u) in enumerate(quarters):
+        part = pl.ds(u * 4, 4)
+        swaps[n].wait_recv()
+        igc[x_to, part] = (igo[x_to, part] + igr[x_to, part].astype(F32)).astype(BF16)
     for r in range(1, 16):
         dx, dq = r // 8, r % 8
         ig_sends.append(
@@ -268,37 +312,40 @@
             )
         )
         go(ig_sends[-1])
-    sum_step(3)
-
-    scale = 8192.0 ** -0.5
-    for k in range(3):
-        sum_send(2, k, 1).wait_recv()
-        sum_send(3, k, 0).wait_recv()
-        total = (
-            pgr[0, 3, k].astype(F32) + pgr[1, 2, k].astype(F32) + pgb[z, k].astype(F32)
-        ) * scale
-        pga[:, k] = total.astype(BF16).reshape(8, 16, B)
+
+    sum_step(1, 0)
+    sum_step(1, 1)
+    products(0, 2, -1, 1)
     pg_sends = []
     for r in range(1, 8):
         pg_sends.append(
             remote(
-                pga.at[lax.rem(q + r, 8)], pgo.at[q], pa_s.at[r], pa_r.at[r], plane(0, r)
+                pgo.at[lax.rem(q + r, 8)], pgp.at[0, q], pa_s.at[0, r], pa_r.at[0, r],
+                plane(0, r),
             )
         )
         go(pg_sends[-1])
-    pgo[q] = pga[q]
-
-    for c in ig_sends:
-        c.wait_recv()
+    pgp[0, q] = pgo[q]
+    sum_step(2, 0)
+    sum_step(2, 1)
+    sum_step(3, 0)
+
     total = igc[xh, q].astype(F32)
     for r in range(1, 16):
+        ig_sends[r - 1].wait_recv()
         total = total + igd[r].astype(F32)
     ig_ref[...] = total.astype(BF16)
 
     for c in pg_sends:
         c.wait_recv()
     for s in range(8):
-        pg_ref[:, :, s * B:(s + 1) * B] = pgo[s]
+        for d in (1, 2):
+            here = pgp.at[d, s]
+            remote(here, here, pa_s.at[d, 0], pa_r.at[d, s], up).wait_recv()
+        total = (
+            pgp[0, s].astype(F32) + pgp[1, s].astype(F32) + pgp[2, s].astype(F32)
+        ) * (8192.0 ** -0.5)
+        pg_ref[:, :, s * B:(s + 1) * B] = total.astype(BF16)
     for c in sent:
         c.wait_send()
 
@@ -312,12 +359,11 @@
             jax.ShapeDtypeStruct((B, 256), BF16),
             jax.ShapeDtypeStruct((3, 16, 1024), BF16),
         ),
-        in_specs=[pl.BlockSpec(memory_space=pl.ANY)] * 4,
+        in_specs=[pl.BlockSpec(memory_space=pltpu.HBM)] * 4,
         out_specs=(vmem, vmem),
         scratch_shapes=[
             pltpu.VMEM((8, 8192 + B), F32),
             pltpu.VMEM((12, 8192), BF16),
-            pltpu.VMEM((64, 1024), BF16),
             pltpu.VMEM((B, 1024), BF16),
             pltpu.VMEM((8, 384, 1024), BF16),
             pltpu.VMEM((8, 2, 8, 64, B), BF16),
@@ -329,27 +375,29 @@
             pltpu.VMEM((1024, 384), BF16),
             pltpu.VMEM((8, 3, B, B), BF16),
             pltpu.VMEM((2, 4, 3, B, B), BF16),
-            pltpu.VMEM((2, 3, 3, B, B), BF16),
+            pltpu.VMEM((2, 2, 3, B, B), BF16),
+            pltpu.VMEM((2, 8, 3, 16, B), BF16),
             pltpu.VMEM((8, 3, 16, B), BF16),
-            pltpu.VMEM((8, 3, 16, B), BF16),
+            pltpu.VMEM((3, 8, 3, 16, B), BF16),
             pltpu.VMEM((2, 8, B, 256), BF16),
             pltpu.VMEM((2, 8, B, 256), BF16),
             pltpu.VMEM((2, 8, B, 256), F32),
             pltpu.VMEM((2, 8, B, 256), BF16),
             pltpu.VMEM((16, B, 256), BF16),
-            dma((8,)), dma((8,)),
+            dma((3, 8)), dma((3, 8)),
             dma((2, 4, 4)), dma((2, 4, 4)),
             dma((8,)), dma((8,)),
+            dma((4,)), dma((4,)),
             dma((8,)), dma((8,)),
             dma, dma,
             dma((8,)),
             dma((2, 4, 3)), dma((2, 4, 3)),
-            dma((8,)), dma((8,)),
-            dma((2,)), dma((2,)),
+            dma((3, 8)), dma((3, 8)),
+            dma((4,)), dma((4,)),
             dma((16,)), dma((16,)),
         ],
         compiler_params=pltpu.CompilerParams(
-            collective_id=0, has_side_effects=True, vmem_limit_bytes=58 * 1024 * 1024
+            collective_id=0, has_side_effects=True, vmem_limit_bytes=48 * 1024 * 1024
         ),
         cost_estimate=pl.CostEstimate(
             flops=6_000_000_000, bytes_accessed=2_000_000, transcendentals=0

time: 60.4 us -> 64.3 us (1.065)
  Pallas kernels: 56.6 us -> 59.4 us
  local copies, waits for them, and re-layouts: 3.01 us -> 4.11 us
    pallas_call x1, Pallas kernels: 56.6 us -> 59.4 us  [per_device(): pl.pallas_call(kernel, out_shape=(jax.ShapeDtypeStruct((B, 256), BF16), j...]
    unnamed x2 -> x8, local copies, waits for them, and re-layouts: 3.01 us -> 4.11 us
where the time goes in v3:
time: 64.3 us; the launch traced here: 64.2 us
  Pallas kernels  59.4 us (92%)
  local copies, waits for them, and re-layouts  4.11 us (6%)
  between operations  0.65 us (1%)
    pallas_call x1, Pallas kernels, per_device(): pl.pallas_call(kernel, out_shape=(jax.ShapeDtypeStruct((B, 256), BF16), j...  59.4 us
    unnamed x8, local copies, waits for them, and re-layouts  4.11 us

profile of v3, /device:TPU:1, one launch (start us, length us, event | category | flops | bytes accessed | tf_op | source)
XLA Modules:
  0.0 64.2 jit_solution(9910772805359967223)
XLA Ops:
  0.6 0.0 copy-start
  0.6 0.9 %copy-done = bf16[128,1024]{1,0:T(8,128)(2,1)S(1)} copy-done((bf16[128,1024]{1,0:T(8,128)(2,1)S(1)}, bf16[128,1024]{1,0:T(8,128)(2,1)}, u32[]{:S(2)}) %copy-start) | copy-done | bytes 262168
  1.6 0.0 copy-start.1
  1.6 0.9 %copy-done.1 = bf16[128,1024]{1,0:T(8,128)(2,1)S(1)} copy-done((bf16[128,1024]{1,0:T(8,128)(2,1)S(1)}, bf16[128,1024]{1,0:T(8,128)(2,1)}, u32[]{:S(2)}) %copy-start.1) | copy-done | bytes 262168
  2.5 0.0 copy-start.2
  2.5 0.9 %copy-done.2 = bf16[12,8192]{1,0:T(8,128)(2,1)S(1)} copy-done((bf16[12,8192]{1,0:T(8,128)(2,1)S(1)}, bf16[12,8192]{1,0:T(8,128)(2,1)}, u32[]{:S(2)}) %copy-start.2) | copy-done | bytes 196632
  3.5 59.4 %shard_map.59 = (bf16[128,256]{1,0:T(8,128)(2,1)S(1)}, bf16[3,16,1024]{2,1,0:T(8,128)(2,1)S(1)}) custom-call(bf16[128,1024]{1,0:T(8,128)(2,1)S(1)} %copy-done, bf16[128,1024]{1,0:T(8,128)(2,1)S(1)} %copy-done.1, bf16[12,8192]{1,0:T(8,128)(2,1)S(1)} %copy-done.2, bf16[3,1024,1024]{2,1,0:T(8,128)(2,1)} %p_ref.1), custom_call_target="tpu_custom_call" | custom-call | flops 6000000000 | bytes 2000000 | tf_op jit(solution)/shard_map/pallas_call | solution.py:356
  62.9 0.6 copy.8
  63.5 0.6 copy.9
Async XLA Ops:
  0.6 1.0 %copy-start = (bf16[128,1024]{1,0:T(8,128)(2,1)S(1)}, bf16[128,1024]{1,0:T(8,128)(2,1)}, u32[]{:S(2)}) copy-start(bf16[128,1024]{1,0:T(8,128)(2,1)} %x_ref.1) | copy-start | bytes 786436
  1.6 0.9 %copy-start.1 = (bf16[128,1024]{1,0:T(8,128)(2,1)S(1)}, bf16[128,1024]{1,0:T(8,128)(2,1)}, u32[]{:S(2)}) copy-start(bf16[128,1024]{1,0:T(8,128)(2,1)} %g_ref.1) | copy-start | bytes 786436
  2.5 0.9 %copy-start.2 = (bf16[12,8192]{1,0:T(8,128)(2,1)S(1)}, bf16[12,8192]{1,0:T(8,128)(2,1)}, u32[]{:S(2)}) copy-start(bf16[12,8192]{1,0:T(8,128)(2,1)} %f_ref.1) | copy-start | bytes 589828

commit v4 on v3

--- a/solution.py
+++ b/solution.py
@@ -16,7 +16,7 @@
 
 def kernel(
     x_ref, g_ref, f_ref, p_ref, ig_ref, pg_ref,
-    taps, fv, xv, hank, gl, g2, acc, corr, xs, xt, pn, pgb, pgr, pgs, pga, pgo, pgp,
+    taps, fv, gv, xv, hank, gl, g2, acc, corr, xs, xt, pn, pgb, pgr, pgs, pga, pgo, pgp,
     igs, igr, igo, igc, igd,
     ga_s, ga_r, gr_s, gr_r, gs_s, gs_r, ge_s, ge_r, xa_s, xa_r, xs_s, xs_r, loc,
     pr_s, pr_r, pa_s, pa_r, is_s, is_r, id_s, id_r,
@@ -60,12 +60,13 @@
     lanes = pl.ds(pl.multiple_of(q * B, B), B)
     f_in = pltpu.make_async_copy(f_ref, fv, loc.at[4])
     g_own = pltpu.make_async_copy(g_ref.at[rows, lanes], gl.at[0, core, q], loc.at[6])
+    g_in = pltpu.make_async_copy(g_ref.at[rows], gv, loc.at[5])
     x_in = pltpu.make_async_copy(x_ref, xv, loc.at[7])
     p_copies = [
         pltpu.make_async_copy(p_ref.at[k, :, lanes], pn.at[:, pl.ds(k * B, B)], loc.at[k])
         for k in range(3)
     ]
-    for c in [f_in, g_own, x_in] + p_copies:
+    for c in [g_in, g_own, f_in, x_in] + p_copies:
         c.start()
     f_in.wait()
     pick = jnp.where(
@@ -99,23 +100,18 @@
         return carry
 
     lax.fori_loop(0, 4, build, 0)
+    g_in.wait()
     g_own.wait()
 
     pl.semaphore_wait(barrier, len(partners))
 
-    pieces = []
-    for r in range(8):
+    a2a = []
+    for r in range(1, 8):
         col = pl.ds(pl.multiple_of(lax.rem(q + r, 8) * B, B), B)
-        for d, dz in ((1, 1), (2, -1), (0, 0)):
-            if r == 0 and dz == 0:
-                continue
-            c = remote(
-                g_ref.at[rows, col], gl.at[-dz % 8, core, q], ga_s.at[d, r],
-                ga_r.at[d, r if dz == 0 else q], near(dz, r),
-            )
-            go(c)
-            if dz == 0:
-                pieces.append(c)
+        a2a.append(
+            remote(gv.at[:, col], gl.at[0, core, q], ga_s.at[r], ga_r.at[r], plane(0, r))
+        )
+        go(a2a[-1])
     lax.fori_loop(4, 8, build, 0)
 
     x_in.wait()
@@ -146,20 +142,12 @@
         other = gl.at[slot, 1 - core]
         return remote(other, other, gs_s.at[slot], gs_r.at[slot], sib)
 
-    def landed(d, m):
-        here = gl.at[-1 % 8 if d == 1 else 1, core, m]
-        return remote(here, here, ga_s.at[d, 0], ga_r.at[d, m], up)
-
-    for c in pieces:
+    for c in a2a:
         c.wait_recv()
-    go(hand_over(0))
     for s in range(4):
         for way in range(2):
-            landed(way + 1, 2 * s).wait_recv()
-            landed(way + 1, 2 * s + 1).wait_recv()
-            go(ring_send(1, s, way))
-    go(hand_over(-1 % 8))
-    go(hand_over(1))
+            go(ring_send(0, s, way))
+    go(hand_over(0))
 
     x_sends = []
     for r in range(1, 8):
@@ -204,7 +192,7 @@
                         ]
 
     conv(0)
-    for step in range(2, 4):
+    for step in range(1, 4):
         for s in range(4):
             for way in range(2):
                 ring_send(step - 1, s, way).wait_recv()
@@ -212,8 +200,9 @@
                     go(ring_send(step, s, way))
         go(hand_over(-step % 8))
         go(hand_over(step))
-        conv(step - 1)
-        conv(1 - step)
+        if step > 1:
+            conv(step - 1)
+            conv(1 - step)
         if step == 3:
             x_own.wait()
             for c in x_sends:
@@ -234,14 +223,20 @@
     def tile(x_to, of_core, upper_half):
         cols = pl.ds(pl.multiple_of(x_to * 512 + of_core * 256, 256), 256)
         return lax.dot_general(
-            corr[upper_half * 512:upper_half * 512 + 512], pn[cols, :],
+            corr[pl.ds(pl.multiple_of(upper_half * 512, 512), 512), :], pn[cols, :],
             (((1,), (1,)), ((), ())), preferred_element_type=F32,
         ).reshape(4, B, 256)
 
-    quarters = [(x_to, u) for u in range(2) for x_to in range(2)]
+    def across(dx, du, dm):
+        m = lax.rem(lax.div(q, 4) + du, 2) * 4 + lax.rem(lax.rem(q, 4) + dm, 4)
+        return lax.rem(xh + dx, 2), m
+
+    quarters = []
+    for dx, du in ((1, 1), (1, 0), (0, 1), (0, 0)):
+        x_to, u = lax.rem(xh + dx, 2), lax.rem(lax.div(q, 4) + du, 2)
+        quarters.append((dx, du, x_to, u, pl.ds(u * 4, 4)))
     swaps = []
-    for n, (x_to, u) in enumerate(quarters):
-        part = pl.ds(u * 4, 4)
+    for n, (dx, du, x_to, u, part) in enumerate(quarters):
         igs[x_to, part] = tile(x_to, 1 - core, u).astype(BF16)
         swaps.append(
             remote(igs.at[x_to, part], igr.at[x_to, part], is_s.at[n], is_r.at[n], sib)
@@ -270,20 +265,19 @@
             up if way == 0 else down,
         )
 
-    def sum_step(step, way):
+    def sum_step(step, k, way):
         last = step == (3 if way == 0 else 2)
         o = 4 - step if way == 0 else step - 3
-        for k in range(3):
-            sum_send(step - 1, k, way).wait_recv()
-            total = (
-                pgr[way, step - 1, k].astype(F32) + pgb[at(o), k].astype(F32)
-            ).astype(BF16)
-            if last:
-                pga[way, :, k] = total.reshape(8, 16, B)
-            else:
-                pgs[way, step - 1, k] = total
-                go(sum_send(step, k, way))
+        sum_send(step - 1, k, way).wait_recv()
+        total = (
+            pgr[way, step - 1, k].astype(F32) + pgb[at(o), k].astype(F32)
+        ).astype(BF16)
         if last:
+            pga[way, :, k] = total.reshape(8, 16, B)
+        else:
+            pgs[way, step - 1, k] = total
+            go(sum_send(step, k, way))
+        if last and k == 2:
             for r in range(8):
                 go(remote(
                     pga.at[way, lax.rem(q + r, 8)], pgp.at[way + 1, q],
@@ -294,28 +288,33 @@
     for k in range(3):
         for way in range(2):
             go(sum_send(0, k, way))
-    for n, (x_to, u) in enumerate(quarters):
-        igo[x_to, u * 4:u * 4 + 4] = tile(x_to, core, u)
     products(3, -2)
+    for dx, du, x_to, u, part in quarters:
+        igo[x_to, part] = tile(x_to, core, u)
 
     ig_sends = []
-    for n, (x_to, u) in enumerate(quarters):
-        part = pl.ds(u * 4, 4)
+
+    def quarter(n):
+        dx, du, x_to, u, part = quarters[n]
         swaps[n].wait_recv()
         igc[x_to, part] = (igo[x_to, part] + igr[x_to, part].astype(F32)).astype(BF16)
-    for r in range(1, 16):
-        dx, dq = r // 8, r % 8
-        ig_sends.append(
-            remote(
-                igc.at[lax.rem(xh + dx, 2), lax.rem(q + dq, 8)], igd.at[r],
-                id_s.at[r], id_r.at[r], plane(dx, dq),
-            )
-        )
-        go(ig_sends[-1])
-
-    sum_step(1, 0)
-    sum_step(1, 1)
-    products(0, 2, -1, 1)
+        for dm in range(4):
+            if dx + du + dm == 0:
+                continue
+            r = dx * 8 + du * 4 + dm
+            to_x, to_m = across(dx, du, dm)
+            ig_sends.append((r, remote(
+                igc.at[to_x, to_m], igd.at[r], id_s.at[r], id_r.at[r],
+                (to_m * 8 + z, to_x * 2 + core),
+            )))
+            go(ig_sends[-1][1])
+
+    for n in range(4):
+        quarter(n)
+    for k in range(3):
+        for way in range(2):
+            sum_step(1, k, way)
+    products(2, -1, 1, 0)
     pg_sends = []
     for r in range(1, 8):
         pg_sends.append(
@@ -326,13 +325,15 @@
         )
         go(pg_sends[-1])
     pgp[0, q] = pgo[q]
-    sum_step(2, 0)
-    sum_step(2, 1)
-    sum_step(3, 0)
+    for k in range(3):
+        for way in range(2):
+            sum_step(2, k, way)
+    for k in range(3):
+        sum_step(3, k, 0)
 
     total = igc[xh, q].astype(F32)
-    for r in range(1, 16):
-        ig_sends[r - 1].wait_recv()
+    for r, c in ig_sends:
+        c.wait_recv()
         total = total + igd[r].astype(F32)
     ig_ref[...] = total.astype(BF16)
 
@@ -359,11 +360,12 @@
             jax.ShapeDtypeStruct((B, 256), BF16),
             jax.ShapeDtypeStruct((3, 16, 1024), BF16),
         ),
-        in_specs=[pl.BlockSpec(memory_space=pltpu.HBM)] * 4,
+        in_specs=[pl.BlockSpec(memory_space=pl.ANY)] * 4,
         out_specs=(vmem, vmem),
         scratch_shapes=[
             pltpu.VMEM((8, 8192 + B), F32),
             pltpu.VMEM((12, 8192), BF16),
+            pltpu.VMEM((64, 1024), BF16),
             pltpu.VMEM((B, 1024), BF16),
             pltpu.VMEM((8, 384, 1024), BF16),
             pltpu.VMEM((8, 2, 8, 64, B), BF16),
@@ -384,7 +386,7 @@
             pltpu.VMEM((2, 8, B, 256), F32),
             pltpu.VMEM((2, 8, B, 256), BF16),
             pltpu.VMEM((16, B, 256), BF16),
-            dma((3, 8)), dma((3, 8)),
+            dma((8,)), dma((8,)),
             dma((2, 4, 4)), dma((2, 4, 4)),
             dma((8,)), dma((8,)),
             dma((4,)), dma((4,)),
@@ -402,7 +404,10 @@
         cost_estimate=pl.CostEstimate(
             flops=6_000_000_000, bytes_accessed=2_000_000, transcendentals=0
         ),
-    )(inputs, cotangent, filters, projections)
+    )(*(
+        pltpu.with_memory_space_constraint(a, pltpu.HBM)
+        for a in (inputs, cotangent, filters, projections)
+    ))
 
 
 def solution(mesh):

time: 64.3 us -> 60.8 us (0.946)
  local copies, waits for them, and re-layouts: 4.11 us -> 1.27 us
    unnamed x8 -> x2, local copies, waits for them, and re-layouts: 4.11 us -> 1.27 us
where the time goes in v4:
time: 60.8 us; the launch traced here: 60.7 us
  Pallas kernels  58.8 us (97%)
  local copies, waits for them, and re-layouts  1.27 us (2%)
  between operations  0.64 us (1%)
    pallas_call x1, Pallas kernels, per_device(): pl.pallas_call(kernel, out_shape=(jax.ShapeDtypeStruct((B, 256), BF16), j...  58.8 us
    unnamed x2, local copies, waits for them, and re-layouts  1.27 us

profile of v4, /device:TPU:1, one launch (start us, length us, event | category | flops | bytes accessed | tf_op | source)
XLA Modules:
  0.0 60.7 jit_solution(5144364251167951606)
XLA Ops:
  0.6 58.8 %shard_map.59 = (bf16[128,256]{1,0:T(8,128)(2,1)S(1)}, bf16[3,16,1024]{2,1,0:T(8,128)(2,1)S(1)}) custom-call(bf16[128,1024]{1,0:T(8,128)(2,1)} %x_ref.1, bf16[128,1024]{1,0:T(8,128)(2,1)} %g_ref.1, bf16[12,8192]{1,0:T(8,128)(2,1)} %f_ref.1, bf16[3,1024,1024]{2,1,0:T(8,128)(2,1)} %p_ref.1), custom_call_target="tpu_custom_call" | custom-call | flops 6000000000 | bytes 2000000 | tf_op jit(solution)/shard_map/pallas_call | solution.py:357
  59.5 0.6 %copy.8 = bf16[128,256]{1,0:T(8,128)(2,1)} copy(bf16[128,256]{1,0:T(8,128)(2,1)S(1)} %get-tuple-element.4) | data formatting | bytes 131072
  60.1 0.6 %copy.9 = bf16[3,16,1024]{2,1,0:T(8,128)(2,1)} copy(bf16[3,16,1024]{2,1,0:T(8,128)(2,1)S(1)} %get-tuple-element.5) | data formatting | bytes 196608

commit v5 on v4

--- a/solution.py
+++ b/solution.py
@@ -17,14 +17,15 @@
 def kernel(
     x_ref, g_ref, f_ref, p_ref, ig_ref, pg_ref,
     taps, fv, gv, xv, hank, gl, g2, acc, corr, xs, xt, pn, pgb, pgr, pgs, pga, pgo, pgp,
-    igs, igr, igo, igc, igd,
+    iga, igb, ra, rb, igt, fa, fb,
     ga_s, ga_r, gr_s, gr_r, gs_s, gs_r, ge_s, ge_r, xa_s, xa_r, xs_s, xs_r, loc,
-    pr_s, pr_r, pa_s, pa_r, is_s, is_r, id_s, id_r,
+    pr_s, pr_r, pa_s, pa_r, pp_s, pp_r, cs_s, cs_r, ip_s, ip_r, iq_s, iq_r,
 ):
     seq = lax.axis_index("seq")
     filt = lax.axis_index("filt")
     q, z = lax.div(seq, 8), lax.rem(seq, 8)
     xh, core = lax.div(filt, 2), lax.rem(filt, 2)
+    x, y = xh * 2 + lax.rem(q, 2), lax.div(q, 2)
     sib = (seq, xh * 2 + 1 - core)
     up = (q * 8 + lax.rem(z + 1, 8), filt)
     down = (q * 8 + lax.rem(z + 7, 8), filt)
@@ -44,13 +45,18 @@
         copy.start()
         sent.append(copy)
 
+    def chip(dx, dy):
+        to_x, to_y = lax.rem(x + dx, 4), lax.rem(y + dy, 4)
+        return ((to_y * 2 + lax.rem(to_x, 2)) * 8 + z, lax.div(to_x, 2) * 2 + core)
+
     def near(dz, dq):
         return (lax.rem(q + dq, 8) * 8 + lax.rem(z + dz + 8, 8), filt)
 
     barrier = pltpu.get_barrier_semaphore()
     partners = (
         [sib]
-        + [plane(r // 8, r % 8) for r in range(1, 16)]
+        + [plane(0, r) for r in range(1, 8)]
+        + [((y * 2 + side) * 8 + z, (1 - xh) * 2 + core) for side in range(2)]
         + [near(dz, r) for dz in (1, -1) for r in range(8)]
     )
     for to in partners:
@@ -58,13 +64,23 @@
 
     rows = pl.ds(pl.multiple_of(core * 64, 64), 64)
     lanes = pl.ds(pl.multiple_of(q * B, B), B)
+    own = pl.ds(pl.multiple_of(core * 384, 128), 384)
+
+    def p_slice(k, to, of_core):
+        e = pl.ds(pl.multiple_of(to * 512 + of_core * 256, 256), 256)
+        return p_ref.at[k, e, lanes]
+
+    def p_place(k, to):
+        return pn.at[to, :, pl.ds(pl.multiple_of(core * 384 + k * B, B), B)]
+
     f_in = pltpu.make_async_copy(f_ref, fv, loc.at[4])
     g_own = pltpu.make_async_copy(g_ref.at[rows, lanes], gl.at[0, core, q], loc.at[6])
     g_in = pltpu.make_async_copy(g_ref.at[rows], gv, loc.at[5])
     x_in = pltpu.make_async_copy(x_ref, xv, loc.at[7])
     p_copies = [
-        pltpu.make_async_copy(p_ref.at[k, :, lanes], pn.at[:, pl.ds(k * B, B)], loc.at[k])
+        pltpu.make_async_copy(p_slice(k, to, core), p_place(k, to), loc.at[8 + 2 * k + to])
         for k in range(3)
+        for to in range(2)
     ]
     for c in [g_in, g_own, f_in, x_in] + p_copies:
         c.start()
@@ -112,6 +128,15 @@
             remote(gv.at[:, col], gl.at[0, core, q], ga_s.at[r], ga_r.at[r], plane(0, r))
         )
         go(a2a[-1])
+    p_sends = [
+        remote(
+            p_slice(k, to, 1 - core), p_place(k, to), pp_s.at[2 * k + to], pp_r.at[2 * k + to], sib
+        )
+        for k in range(3)
+        for to in range(2)
+    ]
+    for c in p_sends:
+        go(c)
     lax.fori_loop(4, 8, build, 0)
 
     x_in.wait()
@@ -155,6 +180,8 @@
             remote(xs.at[half], xt.at[half, :, lanes], xa_s.at[r], xa_r.at[r], plane(0, r))
         )
         go(x_sends[-1])
+
+    corr_sends = []
 
     def conv(o):
         slot = o % 8
@@ -187,9 +214,13 @@
                 done = (acc[p] + term).astype(BF16)
                 for e in range(2):
                     for k in range(3):
-                        corr[(2 * p + e) * B:(2 * p + e + 1) * B, k * B:(k + 1) * B] = done[
-                            k * B:(k + 1) * B, e * B:(e + 1) * B
-                        ]
+                        corr[
+                            (2 * p + e) * B:(2 * p + e + 1) * B,
+                            pl.ds(pl.multiple_of(core * 384 + k * B, B), B),
+                        ] = done[k * B:(k + 1) * B, e * B:(e + 1) * B]
+                mine = corr.at[pl.ds(p * 256, 256), own]
+                corr_sends.append(remote(mine, mine, cs_s.at[p], cs_r.at[p], sib))
+                go(corr_sends[-1])
 
     conv(0)
     for step in range(1, 4):
@@ -217,32 +248,6 @@
     conv(-3)
     conv(4)
 
-    for p in p_copies:
-        p.wait()
-
-    def tile(x_to, of_core, upper_half):
-        cols = pl.ds(pl.multiple_of(x_to * 512 + of_core * 256, 256), 256)
-        return lax.dot_general(
-            corr[pl.ds(pl.multiple_of(upper_half * 512, 512), 512), :], pn[cols, :],
-            (((1,), (1,)), ((), ())), preferred_element_type=F32,
-        ).reshape(4, B, 256)
-
-    def across(dx, du, dm):
-        m = lax.rem(lax.div(q, 4) + du, 2) * 4 + lax.rem(lax.rem(q, 4) + dm, 4)
-        return lax.rem(xh + dx, 2), m
-
-    quarters = []
-    for dx, du in ((1, 1), (1, 0), (0, 1), (0, 0)):
-        x_to, u = lax.rem(xh + dx, 2), lax.rem(lax.div(q, 4) + du, 2)
-        quarters.append((dx, du, x_to, u, pl.ds(u * 4, 4)))
-    swaps = []
-    for n, (dx, du, x_to, u, part) in enumerate(quarters):
-        igs[x_to, part] = tile(x_to, 1 - core, u).astype(BF16)
-        swaps.append(
-            remote(igs.at[x_to, part], igr.at[x_to, part], is_s.at[n], is_r.at[n], sib)
-        )
-        go(swaps[-1])
-
     half_o = pl.ds((1 - core) * 4, 4)
     remote(xt.at[half_o], xt.at[half_o], xs_s, xs_r, sib).wait_recv()
 
@@ -251,7 +256,7 @@
 
     def products(*offsets):
         for o in offsets:
-            part = jnp.dot(xt[at(o)], corr[...], preferred_element_type=F32).astype(BF16)
+            part = jnp.dot(xt[at(o)], corr[:, own], preferred_element_type=F32).astype(BF16)
             for k in range(3):
                 if o == 0:
                     pgo[:, k] = part[:, k * B:(k + 1) * B].reshape(8, 16, B)
@@ -288,29 +293,36 @@
     for k in range(3):
         for way in range(2):
             go(sum_send(0, k, way))
+
+    for c in p_copies:
+        c.wait()
+    for c in p_sends:
+        c.wait_recv()
+    for c in corr_sends:
+        c.wait_recv()
+    ig_sends = []
+    for dy in (2, 1, 3, 0):
+        pair = lax.rem(y + dy, 4)
+        rows_of = corr[pl.ds(pl.multiple_of(pair * 256, 256), 256), :]
+        for to in range(2):
+            part = lax.dot_general(
+                rows_of, pn[to], (((1,), (1,)), ((), ())), preferred_element_type=F32
+            ).astype(BF16)
+            for side in range(2):
+                iga[2 * to + side, pair] = part[side * B:(side + 1) * B, 0:B]
+                igb[pair, 2 * to + side] = part[side * B:(side + 1) * B, B:2 * B]
+        if dy:
+            ig_sends.append(remote(
+                igb.at[pair], rb.at[dy], ip_s.at[1, dy], ip_r.at[1, dy], chip(0, dy)
+            ))
+            go(ig_sends[-1])
+    for dx in (2, 1, 3):
+        ig_sends.append(remote(
+            iga.at[lax.rem(x + dx, 4)], ra.at[dx], ip_s.at[0, dx], ip_r.at[0, dx], chip(dx, 0)
+        ))
+        go(ig_sends[-1])
+
     products(3, -2)
-    for dx, du, x_to, u, part in quarters:
-        igo[x_to, part] = tile(x_to, core, u)
-
-    ig_sends = []
-
-    def quarter(n):
-        dx, du, x_to, u, part = quarters[n]
-        swaps[n].wait_recv()
-        igc[x_to, part] = (igo[x_to, part] + igr[x_to, part].astype(F32)).astype(BF16)
-        for dm in range(4):
-            if dx + du + dm == 0:
-                continue
-            r = dx * 8 + du * 4 + dm
-            to_x, to_m = across(dx, du, dm)
-            ig_sends.append((r, remote(
-                igc.at[to_x, to_m], igd.at[r], id_s.at[r], id_r.at[r],
-                (to_m * 8 + z, to_x * 2 + core),
-            )))
-            go(ig_sends[-1][1])
-
-    for n in range(4):
-        quarter(n)
     for k in range(3):
         for way in range(2):
             sum_step(1, k, way)
@@ -328,14 +340,39 @@
     for k in range(3):
         for way in range(2):
             sum_step(2, k, way)
+
+    for c in ig_sends:
+        c.wait_recv()
+    ig_last = []
+    for d in (2, 1, 3):
+        for mine, got, last, n in ((iga.at[x], ra, fa, 0), (igb.at[y], rb, fb, 1)):
+            there = lax.rem((y if n == 0 else x) + d, 4)
+            total = mine[there].astype(F32)
+            for e in range(1, 4):
+                total = total + got[e, there].astype(F32)
+            out = igt.at[n, d]
+            out[...] = total.astype(BF16)
+            ig_last.append(remote(
+                out, last.at[d], iq_s.at[n, d], iq_r.at[n, d],
+                chip(0, d) if n == 0 else chip(d, 0),
+            ))
+            go(ig_last[-1])
     for k in range(3):
         sum_step(3, k, 0)
 
-    total = igc[xh, q].astype(F32)
-    for r, c in ig_sends:
-        c.wait_recv()
-        total = total + igd[r].astype(F32)
-    ig_ref[...] = total.astype(BF16)
+    halves = []
+    for mine, got, here in ((iga.at[x], ra, y), (igb.at[y], rb, x)):
+        total = mine[here].astype(F32)
+        for e in range(1, 4):
+            total = total + got[e, here].astype(F32)
+        halves.append(total)
+    for c in ig_last:
+        c.wait_recv()
+    for n, last in ((0, fa), (1, fb)):
+        total = halves[n]
+        for e in range(1, 4):
+            total = total + last[e].astype(F32)
+        ig_ref[:, n * B:(n + 1) * B] = total.astype(BF16)
 
     for c in pg_sends:
         c.wait_recv()
@@ -371,32 +408,36 @@
             pltpu.VMEM((8, 2, 8, 64, B), BF16),
             pltpu.VMEM((1, 1152, 256), BF16),
             pltpu.VMEM((4, 384, 256), F32),
-            pltpu.VMEM((1024, 384), BF16),
+            pltpu.VMEM((1024, 768), BF16),
             pltpu.VMEM((8, B, B), BF16),
             pltpu.VMEM((8, B, 1024), BF16),
-            pltpu.VMEM((1024, 384), BF16),
+            pltpu.VMEM((2, 256, 768), BF16),
             pltpu.VMEM((8, 3, B, B), BF16),
             pltpu.VMEM((2, 4, 3, B, B), BF16),
             pltpu.VMEM((2, 2, 3, B, B), BF16),
             pltpu.VMEM((2, 8, 3, 16, B), BF16),
             pltpu.VMEM((8, 3, 16, B), BF16),
             pltpu.VMEM((3, 8, 3, 16, B), BF16),
-            pltpu.VMEM((2, 8, B, 256), BF16),
-            pltpu.VMEM((2, 8, B, 256), BF16),
-            pltpu.VMEM((2, 8, B, 256), F32),
-            pltpu.VMEM((2, 8, B, 256), BF16),
-            pltpu.VMEM((16, B, 256), BF16),
+            pltpu.VMEM((4, 4, B, B), BF16),
+            pltpu.VMEM((4, 4, B, B), BF16),
+            pltpu.VMEM((4, 4, B, B), BF16),
+            pltpu.VMEM((4, 4, B, B), BF16),
+            pltpu.VMEM((2, 4, B, B), BF16),
+            pltpu.VMEM((4, B, B), BF16),
+            pltpu.VMEM((4, B, B), BF16),
             dma((8,)), dma((8,)),
             dma((2, 4, 4)), dma((2, 4, 4)),
             dma((8,)), dma((8,)),
             dma((4,)), dma((4,)),
             dma((8,)), dma((8,)),
             dma, dma,
-            dma((8,)),
+            dma((14,)),
             dma((2, 4, 3)), dma((2, 4, 3)),
             dma((3, 8)), dma((3, 8)),
+            dma((6,)), dma((6,)),
             dma((4,)), dma((4,)),
-            dma((16,)), dma((16,)),
+            dma((2, 4)), dma((2, 4)),
+            dma((2, 4)), dma((2, 4)),
         ],
         compiler_params=pltpu.CompilerParams(
             collective_id=0, has_side_effects=True, vmem_limit_bytes=48 * 1024 * 1024

time: 60.8 us -> 53.2 us (0.88)
  Pallas kernels: 58.8 us -> 51.1 us
    pallas_call x1, Pallas kernels: 58.8 us -> 51.1 us  [per_device(): pl.pallas_call(kernel, out_shape=(jax.ShapeDtypeStruct((B, 256), BF16), j...]
where the time goes in v5:
time: 53.2 us; the launch traced here: 53.1 us
  Pallas kernels  51.1 us (96%)
  local copies, waits for them, and re-layouts  1.27 us (2%)
  between operations  0.64 us (1%)
    pallas_call x1, Pallas kernels, per_device(): pl.pallas_call(kernel, out_shape=(jax.ShapeDtypeStruct((B, 256), BF16), j...  51.1 us
    unnamed x2, local copies, waits for them, and re-layouts  1.27 us

profile of v5, /device:TPU:1, one launch (start us, length us, event | category | flops | bytes accessed | tf_op | source)
XLA Modules:
  0.0 53.1 jit_solution(3880355812064882340)
XLA Ops:
  0.6 51.1 %shard_map.59 = (bf16[128,256]{1,0:T(8,128)(2,1)S(1)}, bf16[3,16,1024]{2,1,0:T(8,128)(2,1)S(1)}) custom-call(bf16[128,1024]{1,0:T(8,128)(2,1)} %x_ref.1, bf16[128,1024]{1,0:T(8,128)(2,1)} %g_ref.1, bf16[12,8192]{1,0:T(8,128)(2,1)} %f_ref.1, bf16[3,1024,1024]{2,1,0:T(8,128)(2,1)} %p_ref.1), custom_call_target="tpu_custom_call" | custom-call | flops 6000000000 | bytes 2000000 | tf_op jit(solution)/shard_map/pallas_call | solution.py:394
  51.8 0.6 %copy.8 = bf16[128,256]{1,0:T(8,128)(2,1)} copy(bf16[128,256]{1,0:T(8,128)(2,1)S(1)} %get-tuple-element.4) | data formatting | bytes 131072
  52.4 0.6 %copy.9 = bf16[3,16,1024]{2,1,0:T(8,128)(2,1)} copy(bf16[3,16,1024]{2,1,0:T(8,128)(2,1)S(1)} %get-tuple-element.5) | data formatting | bytes 196608

commit v6 on v5

--- a/solution.py
+++ b/solution.py
@@ -16,10 +16,10 @@
 
 def kernel(
     x_ref, g_ref, f_ref, p_ref, ig_ref, pg_ref,
-    taps, fv, gv, xv, hank, gl, g2, acc, corr, xs, xt, pn, pgb, pgr, pgs, pga, pgo, pgp,
+    taps, fv, gv, xv, hank, gl, g2, acc, corr, xs, xt, pn, pgb, pgr, pgh, pgs, pga, pgo, pgp,
     iga, igb, ra, rb, igt, fa, fb,
     ga_s, ga_r, gr_s, gr_r, gs_s, gs_r, ge_s, ge_r, xa_s, xa_r, xs_s, xs_r, loc,
-    pr_s, pr_r, pa_s, pa_r, pp_s, pp_r, cs_s, cs_r, ip_s, ip_r, iq_s, iq_r,
+    pr_s, pr_r, ph_s, ph_r, pa_s, pa_r, pp_s, pp_r, cs_s, cs_r, ip_s, ip_r, iq_s, iq_r,
 ):
     seq = lax.axis_index("seq")
     filt = lax.axis_index("filt")
@@ -58,6 +58,7 @@
         + [plane(0, r) for r in range(1, 8)]
         + [((y * 2 + side) * 8 + z, (1 - xh) * 2 + core) for side in range(2)]
         + [near(dz, r) for dz in (1, -1) for r in range(8)]
+        + [near(2, 0), near(-2, 0)]
     )
     for to in partners:
         pl.semaphore_signal(barrier, inc=1, device_id=to, device_id_type=MESH)
@@ -121,13 +122,12 @@
 
     pl.semaphore_wait(barrier, len(partners))
 
-    a2a = []
-    for r in range(1, 8):
-        col = pl.ds(pl.multiple_of(lax.rem(q + r, 8) * B, B), B)
-        a2a.append(
-            remote(gv.at[:, col], gl.at[0, core, q], ga_s.at[r], ga_r.at[r], plane(0, r))
-        )
-        go(a2a[-1])
+    for n, (dy, side) in enumerate(((2, 1), (2, 0), (1, 1), (3, 1), (1, 0), (3, 0), (0, 1))):
+        to_q = lax.rem(y + dy, 4) * 2 + lax.rem(x + side, 2)
+        col = pl.ds(pl.multiple_of(to_q * B, B), B)
+        go(remote(
+            gv.at[:, col], gl.at[0, core, q], ga_s.at[n], ga_r.at[q], (to_q * 8 + z, filt)
+        ))
     p_sends = [
         remote(
             p_slice(k, to, 1 - core), p_place(k, to), pp_s.at[2 * k + to], pp_r.at[2 * k + to], sib
@@ -148,8 +148,11 @@
     x_own = pltpu.make_async_copy(xs.at[half], xt.at[half, :, lanes], loc.at[3])
     x_own.start()
 
+    def turn(s):
+        return lax.rem(y + (0, 1, 3, 2)[s], 4)
+
     def sub(slot, s):
-        return gl.at[slot, core, pl.ds(s * 2, 2)]
+        return gl.at[slot, core, pl.ds(turn(s) * 2, 2)]
 
     def ring_send(step, s, way):
         here = -step % 8 if way == 0 else step
@@ -167,9 +170,15 @@
         other = gl.at[slot, 1 - core]
         return remote(other, other, gs_s.at[slot], gs_r.at[slot], sib)
 
-    for c in a2a:
-        c.wait_recv()
+    def landed(from_q):
+        here = gl.at[0, core, from_q]
+        remote(here, here, ga_s.at[0], ga_r.at[from_q], up).wait_recv()
+
+    landed(lax.div(q, 2) * 2 + lax.rem(q + 1, 2))
     for s in range(4):
+        if s:
+            landed(turn(s) * 2)
+            landed(turn(s) * 2 + 1)
         for way in range(2):
             go(ring_send(0, s, way))
     go(hand_over(0))
@@ -187,7 +196,7 @@
         slot = o % 8
         if o == 4:
             for s in range(4):
-                other = gl.at[4, 1 - core, pl.ds(s * 2, 2)]
+                other = gl.at[4, 1 - core, pl.ds(turn(s) * 2, 2)]
                 remote(other, other, ge_s.at[s], ge_r.at[s], sib).wait_recv()
         else:
             handed(slot).wait_recv()
@@ -264,32 +273,46 @@
                     pgb[at(o), k] = part[:, k * B:(k + 1) * B]
 
     def sum_send(step, k, way):
-        src = pgb.at[at(4 if way == 0 else -3), k] if step == 0 else pgs.at[way, step - 1, k]
+        src = pgb.at[at(3 if way == 0 else -3), k] if step == 0 else pgs.at[way, k]
         return remote(
             src, pgr.at[way, step, k], pr_s.at[way, step, k], pr_r.at[way, step, k],
             up if way == 0 else down,
         )
 
+    def far_send(k, way):
+        return remote(
+            pgb.at[at(4), k, pl.ds(way * 64, 64)], pgh.at[way, k], ph_s.at[way, k],
+            ph_r.at[way, k], near(2 if way == 0 else -2, 0),
+        )
+
     def sum_step(step, k, way):
-        last = step == (3 if way == 0 else 2)
-        o = 4 - step if way == 0 else step - 3
+        o = 3 - step if way == 0 else step - 3
         sum_send(step - 1, k, way).wait_recv()
-        total = (
-            pgr[way, step - 1, k].astype(F32) + pgb[at(o), k].astype(F32)
-        ).astype(BF16)
-        if last:
-            pga[way, :, k] = total.reshape(8, 16, B)
+        total = pgr[way, step - 1, k].astype(F32) + pgb[at(o), k].astype(F32)
+        if step == 1:
+            far_send(k, way).wait_recv()
+            far = pgh[way, k].astype(F32)
+            pgs[way, k, way * 64:way * 64 + 64] = (
+                total[way * 64:way * 64 + 64] + far
+            ).astype(BF16)
+            pgs[way, k, 64 - way * 64:128 - way * 64] = total[
+                64 - way * 64:128 - way * 64
+            ].astype(BF16)
+            go(sum_send(step, k, way))
         else:
-            pgs[way, step - 1, k] = total
-            go(sum_send(step, k, way))
-        if last and k == 2:
+            pga[way, :, k] = total.astype(BF16).reshape(8, 16, B)
+        if step == 2 and k == 2:
             for r in range(8):
                 go(remote(
                     pga.at[way, lax.rem(q + r, 8)], pgp.at[way + 1, q],
                     pa_s.at[way + 1, r], pa_r.at[way + 1, q], near(1 if way == 0 else -1, r),
                 ))
 
-    products(4, -3)
+    products(4)
+    for k in range(3):
+        for way in range(2):
+            go(far_send(k, way))
+    products(3, -3)
     for k in range(3):
         for way in range(2):
             go(sum_send(0, k, way))
@@ -322,11 +345,11 @@
         ))
         go(ig_sends[-1])
 
-    products(3, -2)
+    products(2, -2)
     for k in range(3):
         for way in range(2):
             sum_step(1, k, way)
-    products(2, -1, 1, 0)
+    products(1, -1, 0)
     pg_sends = []
     for r in range(1, 8):
         pg_sends.append(
@@ -357,8 +380,6 @@
                 chip(0, d) if n == 0 else chip(d, 0),
             ))
             go(ig_last[-1])
-    for k in range(3):
-        sum_step(3, k, 0)
 
     halves = []
     for mine, got, here in ((iga.at[x], ra, y), (igb.at[y], rb, x)):
@@ -413,8 +434,9 @@
             pltpu.VMEM((8, B, 1024), BF16),
             pltpu.VMEM((2, 256, 768), BF16),
             pltpu.VMEM((8, 3, B, B), BF16),
-            pltpu.VMEM((2, 4, 3, B, B), BF16),
             pltpu.VMEM((2, 2, 3, B, B), BF16),
+            pltpu.VMEM((2, 3, 64, B), BF16),
+            pltpu.VMEM((2, 3, B, B), BF16),
             pltpu.VMEM((2, 8, 3, 16, B), BF16),
             pltpu.VMEM((8, 3, 16, B), BF16),
             pltpu.VMEM((3, 8, 3, 16, B), BF16),
@@ -432,7 +454,8 @@
             dma((8,)), dma((8,)),
             dma, dma,
             dma((14,)),
-            dma((2, 4, 3)), dma((2, 4, 3)),
+            dma((2, 2, 3)), dma((2, 2, 3)),
+            dma((2, 3)), dma((2, 3)),
             dma((3, 8)), dma((3, 8)),
             dma((6,)), dma((6,)),
             dma((4,)), dma((4,)),

time: 53.2 us -> 53.3 us (level)
  no operation moved by 1% of the time
where the time goes in v6:
time: 53.3 us; the launch traced here: 53.2 us
  Pallas kernels  51.3 us (96%)
  local copies, waits for them, and re-layouts  1.27 us (2%)
  between operations  0.64 us (1%)
    pallas_call x1, Pallas kernels, per_device(): pl.pallas_call(kernel, out_shape=(jax.ShapeDtypeStruct((B, 256), BF16), j...  51.3 us
    unnamed x2, local copies, waits for them, and re-layouts  1.27 us

profile of v6, /device:TPU:1, one launch (start us, length us, event | category | flops | bytes accessed | tf_op | source)
XLA Modules:
  0.0 53.2 jit_solution(7230002818106683200)
XLA Ops:
  0.6 51.3 %shard_map.59 = (bf16[128,256]{1,0:T(8,128)(2,1)S(1)}, bf16[3,16,1024]{2,1,0:T(8,128)(2,1)S(1)}) custom-call(bf16[128,1024]{1,0:T(8,128)(2,1)} %x_ref.1, bf16[128,1024]{1,0:T(8,128)(2,1)} %g_ref.1, bf16[12,8192]{1,0:T(8,128)(2,1)} %f_ref.1, bf16[3,1024,1024]{2,1,0:T(8,128)(2,1)} %p_ref.1), custom_call_target="tpu_custom_call" | custom-call | flops 6000000000 | bytes 2000000 | tf_op jit(solution)/shard_map/pallas_call | solution.py:415
  51.9 0.6 %copy.8 = bf16[128,256]{1,0:T(8,128)(2,1)} copy(bf16[128,256]{1,0:T(8,128)(2,1)S(1)} %get-tuple-element.4) | data formatting | bytes 131072
  52.6 0.6 %copy.9 = bf16[3,16,1024]{2,1,0:T(8,128)(2,1)} copy(bf16[3,16,1024]{2,1,0:T(8,128)(2,1)S(1)} %get-tuple-element.5) | data formatting | bytes 196608

commit v7 on v6

--- a/solution.py
+++ b/solution.py
@@ -45,6 +45,11 @@
         copy.start()
         sent.append(copy)
 
+    def settle(count):
+        for c in sent[:count]:
+            c.wait_send()
+        del sent[:count]
+
     def chip(dx, dy):
         to_x, to_y = lax.rem(x + dx, 4), lax.rem(y + dy, 4)
         return ((to_y * 2 + lax.rem(to_x, 2)) * 8 + z, lax.div(to_x, 2) * 2 + core)
@@ -54,11 +59,9 @@
 
     barrier = pltpu.get_barrier_semaphore()
     partners = (
-        [sib]
-        + [plane(0, r) for r in range(1, 8)]
+        [plane(0, r) for r in range(1, 8)]
         + [((y * 2 + side) * 8 + z, (1 - xh) * 2 + core) for side in range(2)]
-        + [near(dz, r) for dz in (1, -1) for r in range(8)]
-        + [near(2, 0), near(-2, 0)]
+        + [up, down, sib]
     )
     for to in partners:
         pl.semaphore_signal(barrier, inc=1, device_id=to, device_id_type=MESH)
@@ -249,6 +252,7 @@
                 c.wait_recv()
             x_hand = remote(xt.at[half], xt.at[half], xs_s, xs_r, sib)
             go(x_hand)
+    early = len(sent)
     conv(3)
     for s in range(4):
         ring_send(3, s, s // 2).wait_recv()
@@ -346,6 +350,7 @@
         go(ig_sends[-1])
 
     products(2, -2)
+    settle(early)
     for k in range(3):
         for way in range(2):
             sum_step(1, k, way)
@@ -364,6 +369,7 @@
         for way in range(2):
             sum_step(2, k, way)
 
+    middle = len(sent) - 23
     for c in ig_sends:
         c.wait_recv()
     ig_last = []
@@ -381,6 +387,7 @@
             ))
             go(ig_last[-1])
 
+    settle(middle)
     halves = []
     for mine, got, here in ((iga.at[x], ra, y), (igb.at[y], rb, x)):
         total = mine[here].astype(F32)
@@ -405,8 +412,7 @@
             pgp[0, s].astype(F32) + pgp[1, s].astype(F32) + pgp[2, s].astype(F32)
         ) * (8192.0 ** -0.5)
         pg_ref[:, :, s * B:(s + 1) * B] = total.astype(BF16)
-    for c in sent:
-        c.wait_send()
+    settle(len(sent))
 
 
 def per_device(inputs, cotangent, filters, projections):

time: 53.3 us -> 50.9 us (0.955)
  Pallas kernels: 51.3 us -> 48.9 us
    pallas_call x1, Pallas kernels: 51.3 us -> 48.9 us  [per_device(): pl.pallas_call(kernel, out_shape=(jax.ShapeDtypeStruct((B, 256), BF16), j...]
where the time goes in v7:
time: 50.9 us; the launch traced here: 50.8 us
  Pallas kernels  48.9 us (96%)
  local copies, waits for them, and re-layouts  1.27 us (2%)
  between operations  0.64 us (1%)
    pallas_call x1, Pallas kernels, per_device(): pl.pallas_call(kernel, out_shape=(jax.ShapeDtypeStruct((B, 256), BF16), j...  48.9 us
    unnamed x2, local copies, waits for them, and re-layouts  1.27 us

profile of v7, /device:TPU:1, one launch (start us, length us, event | category | flops | bytes accessed | tf_op | source)
XLA Modules:
  0.0 50.8 jit_solution(10381024821065298837)
XLA Ops:
  0.6 48.9 %shard_map.59 = (bf16[128,256]{1,0:T(8,128)(2,1)S(1)}, bf16[3,16,1024]{2,1,0:T(8,128)(2,1)S(1)}) custom-call(bf16[128,1024]{1,0:T(8,128)(2,1)} %x_ref.1, bf16[128,1024]{1,0:T(8,128)(2,1)} %g_ref.1, bf16[12,8192]{1,0:T(8,128)(2,1)} %f_ref.1, bf16[3,1024,1024]{2,1,0:T(8,128)(2,1)} %p_ref.1), custom_call_target="tpu_custom_call" | custom-call | flops 6000000000 | bytes 2000000 | tf_op jit(solution)/shard_map/pallas_call | solution.py:421
  49.5 0.6 %copy.8 = bf16[128,256]{1,0:T(8,128)(2,1)} copy(bf16[128,256]{1,0:T(8,128)(2,1)S(1)} %get-tuple-element.4) | data formatting | bytes 131072
  50.1 0.6 %copy.9 = bf16[3,16,1024]{2,1,0:T(8,128)(2,1)} copy(bf16[3,16,1024]{2,1,0:T(8,128)(2,1)S(1)} %get-tuple-element.5) | data formatting | bytes 196608

commit v8 on v7

--- a/solution.py
+++ b/solution.py
@@ -312,13 +312,10 @@
                     pa_s.at[way + 1, r], pa_r.at[way + 1, q], near(1 if way == 0 else -1, r),
                 ))
 
-    products(4)
+    products(4, 3, -3)
     for k in range(3):
         for way in range(2):
             go(far_send(k, way))
-    products(3, -3)
-    for k in range(3):
-        for way in range(2):
             go(sum_send(0, k, way))
 
     for c in p_copies:

time: 50.9 us -> 51.2 us (level)
  no operation moved by 1% of the time
where the time goes in v8:
time: 51.2 us; the launch traced here: 51.1 us
  Pallas kernels  49.1 us (96%)
  local copies, waits for them, and re-layouts  1.27 us (2%)
  between operations  0.64 us (1%)
    pallas_call x1, Pallas kernels, per_device(): pl.pallas_call(kernel, out_shape=(jax.ShapeDtypeStruct((B, 256), BF16), j...  49.1 us
    unnamed x2, local copies, waits for them, and re-layouts  1.27 us

profile of v8, /device:TPU:1, one launch (start us, length us, event | category | flops | bytes accessed | tf_op | source)
XLA Modules:
  0.0 51.1 jit_solution(4126937129331195333)
XLA Ops:
  0.6 49.1 %shard_map.59 = (bf16[128,256]{1,0:T(8,128)(2,1)S(1)}, bf16[3,16,1024]{2,1,0:T(8,128)(2,1)S(1)}) custom-call(bf16[128,1024]{1,0:T(8,128)(2,1)} %x_ref.1, bf16[128,1024]{1,0:T(8,128)(2,1)} %g_ref.1, bf16[12,8192]{1,0:T(8,128)(2,1)} %f_ref.1, bf16[3,1024,1024]{2,1,0:T(8,128)(2,1)} %p_ref.1), custom_call_target="tpu_custom_call" | custom-call | flops 6000000000 | bytes 2000000 | tf_op jit(solution)/shard_map/pallas_call | solution.py:418
  49.8 0.6 %copy.8 = bf16[128,256]{1,0:T(8,128)(2,1)} copy(bf16[128,256]{1,0:T(8,128)(2,1)S(1)} %get-tuple-element.4) | data formatting | bytes 131072
  50.4 0.6 %copy.9 = bf16[3,16,1024]{2,1,0:T(8,128)(2,1)} copy(bf16[3,16,1024]{2,1,0:T(8,128)(2,1)S(1)} %get-tuple-element.5) | data formatting | bytes 196608

commit v9 on v7

--- a/solution.py
+++ b/solution.py
@@ -350,10 +350,10 @@
         go(ig_sends[-1])
 
     products(2, -2)
-    settle(early)
     for k in range(3):
         for way in range(2):
             sum_step(1, k, way)
+    settle(early)
     products(1, -1, 0)
     pg_sends = []
     for r in range(1, 8):

time: 50.9 us -> 50.9 us (level)
  no operation moved by 1% of the time
where the time goes in v9:
time: 50.9 us; the launch traced here: 50.8 us
  Pallas kernels  48.9 us (96%)
  local copies, waits for them, and re-layouts  1.27 us (2%)
  between operations  0.64 us (1%)
    pallas_call x1, Pallas kernels, per_device(): pl.pallas_call(kernel, out_shape=(jax.ShapeDtypeStruct((B, 256), BF16), j...  48.9 us
    unnamed x2, local copies, waits for them, and re-layouts  1.27 us

profile of v9, /device:TPU:1, one launch (start us, length us, event | category | flops | bytes accessed | tf_op | source)
XLA Modules:
  0.0 50.8 jit_solution(13495957283878083817)
XLA Ops:
  0.6 48.9 %shard_map.59 = (bf16[128,256]{1,0:T(8,128)(2,1)S(1)}, bf16[3,16,1024]{2,1,0:T(8,128)(2,1)S(1)}) custom-call(bf16[128,1024]{1,0:T(8,128)(2,1)} %x_ref.1, bf16[128,1024]{1,0:T(8,128)(2,1)} %g_ref.1, bf16[12,8192]{1,0:T(8,128)(2,1)} %f_ref.1, bf16[3,1024,1024]{2,1,0:T(8,128)(2,1)} %p_ref.1), custom_call_target="tpu_custom_call" | custom-call | flops 6000000000 | bytes 2000000 | tf_op jit(solution)/shard_map/pallas_call | solution.py:421
  49.5 0.6 %copy.8 = bf16[128,256]{1,0:T(8,128)(2,1)} copy(bf16[128,256]{1,0:T(8,128)(2,1)S(1)} %get-tuple-element.4) | data formatting | bytes 131072
  50.1 0.6 %copy.9 = bf16[3,16,1024]{2,1,0:T(8,128)(2,1)} copy(bf16[3,16,1024]{2,1,0:T(8,128)(2,1)S(1)} %get-tuple-element.5) | data formatting | bytes 196608

commit v10 on v9

--- a/solution.py
+++ b/solution.py
@@ -312,14 +312,15 @@
                     pa_s.at[way + 1, r], pa_r.at[way + 1, q], near(1 if way == 0 else -1, r),
                 ))
 
+    products(3, -3)
+    for way in range(2):
+        go(sum_send(0, 0, way))
     products(4)
     for k in range(3):
         for way in range(2):
             go(far_send(k, way))
-    products(3, -3)
-    for k in range(3):
-        for way in range(2):
-            go(sum_send(0, k, way))
+            if k:
+                go(sum_send(0, k, way))
 
     for c in p_copies:
         c.wait()

time: 50.9 us -> 51.2 us (level)
  no operation moved by 1% of the time
where the time goes in v10:
time: 51.2 us; the launch traced here: 51.1 us
  Pallas kernels  49.1 us (96%)
  local copies, waits for them, and re-layouts  1.27 us (2%)
  between operations  0.64 us (1%)
    pallas_call x1, Pallas kernels, per_device(): pl.pallas_call(kernel, out_shape=(jax.ShapeDtypeStruct((B, 256), BF16), j...  49.1 us
    unnamed x2, local copies, waits for them, and re-layouts  1.27 us

profile of v10, /device:TPU:1, one launch (start us, length us, event | category | flops | bytes accessed | tf_op | source)
XLA Modules:
  0.0 51.1 jit_solution(16145575513529470287)
XLA Ops:
  0.6 49.1 %shard_map.59 = (bf16[128,256]{1,0:T(8,128)(2,1)S(1)}, bf16[3,16,1024]{2,1,0:T(8,128)(2,1)S(1)}) custom-call(bf16[128,1024]{1,0:T(8,128)(2,1)} %x_ref.1, bf16[128,1024]{1,0:T(8,128)(2,1)} %g_ref.1, bf16[12,8192]{1,0:T(8,128)(2,1)} %f_ref.1, bf16[3,1024,1024]{2,1,0:T(8,128)(2,1)} %p_ref.1), custom_call_target="tpu_custom_call" | custom-call | flops 6000000000 | bytes 2000000 | tf_op jit(solution)/shard_map/pallas_call | solution.py:422
  49.8 0.6 %copy.8 = bf16[128,256]{1,0:T(8,128)(2,1)} copy(bf16[128,256]{1,0:T(8,128)(2,1)S(1)} %get-tuple-element.4) | data formatting | bytes 131072
  50.4 0.6 %copy.9 = bf16[3,16,1024]{2,1,0:T(8,128)(2,1)} copy(bf16[3,16,1024]{2,1,0:T(8,128)(2,1)S(1)} %get-tuple-element.5) | data formatting | bytes 196608
